TPU v7x, 256 devices: a whole 4x4x8 slice. The times are simulated.
256 devices in a mesh: gx: 8 (over y_lo, x), gy: 4 (over y_hi, core), gz: 8 (over z).
Axes of the slice: x: 4, y: 4 (y_hi: 2, y_lo: 2; y = y_hi * 2 + y_lo), z: 8, core: 2. Of those that a mesh axis runs over, the one named last changes fastest.
Arguments:
- density: float32 [256, 128, 2048], P('gx', 'gy', 'gz'), may hold values from 0 to 1
- voxel_kind: int32 [256, 128, 2048], P('gx', 'gy', 'gz'), may hold values from 0 to 3
- velocity: float32 [3, 256, 128, 2048], P(None, 'gx', 'gy', 'gz'), may hold values from -6 to 6
- adjoint: float32 [4, 256, 128, 2048], P(None, 'gx', 'gy', 'gz'), may hold values from -6 to 6
Outputs:
- adjoint_residual: float32 [4, 256, 128, 2048], P(None, 'gx', 'gy', 'gz')
- sensitivity: float32 [256, 128, 2048], P('gx', 'gy', 'gz')
All inputs are finite; a program needn't handle non-finite values.
Results may differ from a plain program's by a relative error of at most 0.0003.
Values sent between devices are 32-bit elements; how exact they have to be, the bound alone decides.
A program may use at most 192 MiB of HBM per device.

v0:
```python
import math

import jax
import jax.numpy as jnp
from jax import lax
from jax.sharding import PartitionSpec as P

taps_list = [(7.0 - abs(k)) / 49.0 for k in range(-6, 7)]
proj_denom = 2.0 * math.tanh(2.0)


def extended(value, sides, width):
    for axis, dim in sides:
        size, length = (lax.axis_size(axis), value.shape[dim])
        up = [(i, (i + 1) % size) for i in range(size - 1)]
        down = [(j, i) for i, j in up]
        last = lax.slice_in_dim(value, length - width, length, axis=dim)
        first = lax.slice_in_dim(value, 0, width, axis=dim)
        before = lax.ppermute(last, axis, up)
        after = lax.ppermute(first, axis, down)
        value = jnp.concatenate([before, value, after], axis=dim)
    return value


def smooth_axis(field, dim, count):
    total = jnp.zeros(field.shape[:dim] + (count,) + field.shape[dim + 1 :], field.dtype)
    for k in range(13):
        total = total + taps_list[k] * lax.slice_in_dim(field, k, k + count, axis=dim)
    return total


def filter_field(field):
    sizes_here = field.shape
    padded = extended(field, (("gx", 0),), 6)
    first = smooth_axis(padded, 0, sizes_here[0])
    padded = extended(first, (("gy", 1),), 6)
    second = smooth_axis(padded, 1, sizes_here[1])
    padded = extended(second, (("gz", 2),), 6)
    return smooth_axis(padded, 2, sizes_here[2])


def stencils(padded):
    center = padded[..., 1:-1, 1:-1, 1:-1]
    xplus = padded[..., 2:, 1:-1, 1:-1]
    xminus = padded[..., :-2, 1:-1, 1:-1]
    yplus = padded[..., 1:-1, 2:, 1:-1]
    yminus = padded[..., 1:-1, :-2, 1:-1]
    zplus = padded[..., 1:-1, 1:-1, 2:]
    zminus = padded[..., 1:-1, 1:-1, :-2]
    laplace = xplus + xminus + yplus + yminus + zplus + zminus - 6.0 * center
    grads = ((xplus - xminus) * 0.5, (yplus - yminus) * 0.5, (zplus - zminus) * 0.5)
    return (center, laplace, grads)


def design_terms(rho_filt, voxel_kind, flow_pad, adj_pad):
    design = voxel_kind == 0
    solid = voxel_kind == 1
    inlet = voxel_kind == 2
    outlet = voxel_kind == 3
    tanh_part = jnp.tanh(4.0 * (rho_filt - 0.5))
    proj = (math.tanh(2.0) + tanh_part) / proj_denom
    rho_proj = jnp.where(design, proj, jnp.where(solid, 0.0, 1.0))
    alpha = 2.0 * (1.0 - rho_proj) / (1.0 + rho_proj)
    flow_c, flow_lap, unused_a = stencils(flow_pad)
    lam_c, lam_lap, lam_grads = stencils(adj_pad[:3])
    mu_c, unused_b, mu_grads = stencils(adj_pad[3])
    mu_grad = jnp.stack(mu_grads, 0)
    momentum = -lam_lap + alpha * lam_c - mu_grad + 2.0 * alpha * flow_c - 2.0 * flow_lap
    momentum = jnp.where(inlet, lam_c, momentum)
    div_lam = lam_grads[0][0] + lam_grads[1][1] + lam_grads[2][2]
    continuity = jnp.where(outlet, mu_c, -div_lam)
    residual = jnp.concatenate([momentum, continuity[None]], 0)
    d_alpha = -4.0 / ((1.0 + rho_proj) * (1.0 + rho_proj))
    d_proj = 4.0 * (1.0 - tanh_part * tanh_part) / proj_denom
    energy = jnp.sum(flow_c * flow_c, 0) + jnp.sum(flow_c * lam_c, 0)
    pointwise = jnp.where(design, d_alpha * energy * d_proj, 0.0)
    return (residual, pointwise)


def body(density, voxel_kind, velocity, adjoint):
    flow_pad, adj_pad = (
        extended(velocity, (("gx", 1), ("gy", 2), ("gz", 3)), 1),
        extended(adjoint, (("gx", 1), ("gy", 2), ("gz", 3)), 1),
    )
    rho_filt = filter_field(density)
    residual, pointwise = design_terms(rho_filt, voxel_kind, flow_pad, adj_pad)
    return (residual, filter_field(pointwise))


def solution(mesh):
    return jax.shard_map(
        body,
        mesh=mesh,
        in_specs=(
            P("gx", "gy", "gz"),
            P("gx", "gy", "gz"),
            P(None, "gx", "gy", "gz"),
            P(None, "gx", "gy", "gz"),
        ),
        out_specs=(P(None, "gx", "gy", "gz"), P("gx", "gy", "gz")),
        check_vma=False,
    )
```

profile of v0, /device:TPU:9, one launch (start us, length us, event | category | flops | bytes accessed | tf_op | source)
XLA Modules:
  0.0 207.2 jit_solution(10732798103360918456)
XLA Ops:
  1.9 3.1 %collective-permute-start.6 = (f32[6,32,256]{2,1,0:T(8,128)S(1)}, f32[6,32,256]{2,1,0:T(8,128)S(1)}, u32[]{:S(2)}, u32[]{:S(2)}) collective-permute-start(f32[6,32,256]{2,1,0:T(8,128)S(1)} %get-tuple-element.43), channel_id=1, source_target_pairs={{0,32},{32,64},{64,96},{96,128},{128,160},{160,192},{192,224},{1,3... | collective-permute-start | bytes 589832 | tf_op jit(solution)/shard_map/ppermute | solution.py:19
  5.0 4.3 %collective-permute-start.7 = (f32[6,32,256]{2,1,0:T(8,128)S(1)}, f32[6,32,256]{2,1,0:T(8,128)S(1)}, u32[]{:S(2)}, u32[]{:S(2)}) collective-permute-start(f32[6,32,256]{2,1,0:T(8,128)S(1)} %get-tuple-element.44), channel_id=1, source_target_pairs={{32,0},{64,32},{96,64},{128,96},{160,128},{192,160},{224,192},{33,... | collective-permute-start | bytes 589832 | tf_op jit(solution)/shard_map/ppermute | solution.py:20
  10.2 1.9 collective-permute-start.13
  13.2 2.2 %collective-permute-start.1 = (f32[4,1,32,256]{3,2,1,0:T(8,128)S(1)}, f32[4,1,32,256]{3,2,1,0:T(8,128)S(1)}, u32[]{:S(2)}, u32[]{:S(2)}) collective-permute-start(f32[4,1,32,256]{3,2,1,0:T(8,128)S(1)} %get-tuple-element.17), channel_id=1, source_target_pairs={{0,32},{32,64},{64,96},{96,128},{128,160},{160,192},{192,224},{1,3... | collective-permute-start | bytes 393224 | tf_op jit(solution)/shard_map/ppermute | solution.py:19
  15.4 5.2 %collective-permute-start = (f32[4,1,32,256]{3,2,1,0:T(8,128)S(1)}, f32[4,1,32,256]{3,2,1,0:T(8,128)S(1)}, u32[]{:S(2)}, u32[]{:S(2)}) collective-permute-start(f32[4,1,32,256]{3,2,1,0:T(8,128)S(1)} %get-tuple-element.16), channel_id=1, source_target_pairs={{32,0},{64,32},{96,64},{128,96},{160,128},{192,160},{224,192},{33,... | collective-permute-start | bytes 393224 | tf_op jit(solution)/shard_map/ppermute | solution.py:20
  20.6 2.1 broadcast_compare_fusion.1
  22.6 3.4 %collective-permute-start.12 = (f32[3,1,32,256]{3,2,1,0:T(8,128)S(1)}, f32[3,1,32,256]{3,2,1,0:T(8,128)S(1)}, u32[]{:S(2)}, u32[]{:S(2)}) collective-permute-start(f32[3,1,32,256]{3,2,1,0:T(8,128)S(1)} %get-tuple-element.23), channel_id=1, source_target_pairs={{32,0},{64,32},{96,64},{128,96},{160,128},{192,160},{224,192},{33,... | collective-permute-start | bytes 294920 | tf_op jit(solution)/shard_map/ppermute | solution.py:20
  26.0 4.6 %multiply_reduce_fusion = (f32[32,32,256]{2,1,0:T(8,128)}, f32[32,32,256]{2,1,0:T(8,128)}, f32[3,34,32,256]{3,2,1,0:T(8,128)S(1)}) fusion(f32[3,32,32,256]{3,2,1,0:T(8,128)S(1)} %copy-done.6, f32[4,32,32,256]{3,2,1,0:T(8,128)} %param.7, f32[3,34,32,256]{3,2,1,0:T(8,128)S(1)} %constant_dynamic-update-slice_fusion.9), kind=kLoop, calls=%fused_computation.66 | loop fusion | flops 2621440 | bytes 11534336 | tf_op jit(solution)/shard_map/reduce_sum | solution.py:75
  30.9 4.3 %collective-permute-start.14 = (f32[3,34,1,256]{3,2,1,0:T(1,128)S(1)}, f32[3,34,1,256]{3,2,1,0:T(1,128)S(1)}, u32[]{:S(2)}, u32[]{:S(2)}) collective-permute-start(f32[3,34,1,256]{3,2,1,0:T(1,128)S(1)} %get-tuple-element.21), channel_id=1, source_target_pairs={{8,0},{16,8},{24,16},{9,1},{17,9},{25,17},{10,2},{18,10},{26,18},{... | collective-permute-start | bytes 313352 | tf_op jit(solution)/shard_map/ppermute | solution.py:20
  35.1 3.8 %collective-permute-start.15 = (f32[3,34,1,256]{3,2,1,0:T(1,128)S(1)}, f32[3,34,1,256]{3,2,1,0:T(1,128)S(1)}, u32[]{:S(2)}, u32[]{:S(2)}) collective-permute-start(f32[3,34,1,256]{3,2,1,0:T(1,128)S(1)} %get-tuple-element.20), channel_id=1, source_target_pairs={{0,8},{8,16},{16,24},{1,9},{9,17},{17,25},{2,10},{10,18},{18,26},{... | collective-permute-start | bytes 313352 | tf_op jit(solution)/shard_map/ppermute | solution.py:19
  39.8 2.1 copy-done
  42.1 1.9 collective-permute-start.2
  44.0 5.1 %collective-permute-start.3 = (f32[4,34,1,256]{3,2,1,0:T(1,128)S(1)}, f32[4,34,1,256]{3,2,1,0:T(1,128)S(1)}, u32[]{:S(2)}, u32[]{:S(2)}) collective-permute-start(f32[4,34,1,256]{3,2,1,0:T(1,128)S(1)} %get-tuple-element.14), channel_id=1, source_target_pairs={{0,8},{8,16},{16,24},{1,9},{9,17},{17,25},{2,10},{10,18},{18,26},{... | collective-permute-start | bytes 417800 | tf_op jit(solution)/shard_map/ppermute | solution.py:19
  49.5 1.9 fusion.214
  52.2 2.0 fusion.230
  54.2 3.0 %copy.38 = f32[3,34,34,1]{2,3,1,0:T(1,128)} copy(f32[3,34,34,1]{3,2,1,0:T(8,128)} %get-tuple-element.18) | data formatting | bytes 27744 | tf_op jit(solution)/shard_map/slice | solution.py:18
  59.3 4.2 %collective-permute-start.17 = (f32[3,34,34,1]{2,3,1,0:T(1,128)S(1)}, f32[3,34,34,1]{2,3,1,0:T(1,128)S(1)}, u32[]{:S(2)}, u32[]{:S(2)}) collective-permute-start(f32[3,34,34,1]{2,3,1,0:T(1,128)S(1)} %copy.40), channel_id=1, source_target_pairs={{0,1},{1,2},{2,3},{3,4},{4,5},{5,6},{6,7},{8,9},{9,10},{10,11},{11... | collective-permute-start | bytes 41624 | tf_op jit(solution)/shard_map/ppermute | solution.py:19
  63.5 3.1 %pad_maximum_fusion = f32[4,34,34,256]{3,2,1,0:T(8,128)S(1)} fusion(f32[4,34,1,256]{3,2,1,0:T(1,128)S(1)} %collective-permute-done.2, f32[4,34,32,256]{3,2,1,0:T(8,128)} %copy-done, f32[4,34,1,256]{3,2,1,0:T(1,128)S(1)} %collective-permute-done.3), kind=kLoop, calls=%fused_computation | loop fusion | flops 2367488 | bytes 9469952 | tf_op jit(solution)/shard_map/concatenate | solution.py:21
  66.6 2.4 %fusion.227 = (f32[4,34,34,1]{3,2,1,0:T(8,128)}, f32[4,34,34,1]{3,2,1,0:T(8,128)S(1)}) fusion(f32[4,34,34,256]{3,2,1,0:T(8,128)S(1)} %pad_maximum_fusion), kind=kLoop, calls=%fused_computation.405 | loop fusion | bytes 73984 | tf_op jit(solution)/shard_map/slice | solution.py:18
  69.0 2.8 %copy.32 = f32[4,34,34,1]{2,0,3,1:T(4,128)S(1)} copy(f32[4,34,34,1]{3,2,1,0:T(8,128)} %get-tuple-element.10) | data formatting | bytes 36992 | tf_op jit(solution)/shard_map/slice | solution.py:18
  73.2 1.7 copy.34
  74.8 4.8 %collective-permute-start.5 = (f32[4,34,34,1]{2,0,3,1:T(4,128)}, f32[4,34,34,1]{2,0,3,1:T(4,128)}, u32[]{:S(2)}, u32[]{:S(2)}) collective-permute-start(f32[4,34,34,1]{2,0,3,1:T(4,128)} %copy.34), channel_id=1, source_target_pairs={{0,1},{1,2},{2,3},{3,4},{4,5},{5,6},{6,7},{8,9},{9,10},{10,11},{11... | collective-permute-start | bytes 55496 | tf_op jit(solution)/shard_map/ppermute | solution.py:19
  79.6 1.9 fusion.237
  81.5 2.7 %collective-permute-start.8 = (f32[32,6,256]{2,1,0:T(8,128)}, f32[32,6,256]{2,1,0:T(8,128)}, u32[]{:S(2)}, u32[]{:S(2)}) collective-permute-start(f32[32,6,256]{2,1,0:T(8,128)} %get-tuple-element.39), channel_id=1, source_target_pairs={{0,8},{8,16},{16,24},{1,9},{9,17},{17,25},{2,10},{10,18},{18,26},{... | collective-permute-start | bytes 589832 | tf_op jit(solution)/shard_map/ppermute | solution.py:19
  84.2 2.5 %collective-permute-start.9 = (f32[32,6,256]{2,1,0:T(8,128)}, f32[32,6,256]{2,1,0:T(8,128)}, u32[]{:S(2)}, u32[]{:S(2)}) collective-permute-start(f32[32,6,256]{2,1,0:T(8,128)} %get-tuple-element.40), channel_id=1, source_target_pairs={{8,0},{16,8},{24,16},{9,1},{17,9},{25,17},{10,2},{18,10},{26,18},{... | collective-permute-start | bytes 589832 | tf_op jit(solution)/shard_map/ppermute | solution.py:20
  86.7 2.1 %copy.39 = f32[3,34,34,1]{3,2,1,0:T(8,128)} copy(f32[3,34,34,1]{2,3,1,0:T(1,128)S(1)} %collective-permute-done.16) | data formatting | bytes 27744 | tf_op jit(solution)/shard_map/ppermute | solution.py:20
  88.9 2.3 %copy.41 = f32[3,34,34,1]{3,2,1,0:T(8,128)} copy(f32[3,34,34,1]{2,3,1,0:T(1,128)S(1)} %collective-permute-done.17) | data formatting | bytes 27744 | tf_op jit(solution)/shard_map/ppermute | solution.py:19
  91.1 1.9 copy.33
  93.1 3.6 %copy.35 = f32[4,34,34,1]{3,2,1,0:T(8,128)} copy(f32[4,34,34,1]{2,0,3,1:T(4,128)} %collective-permute-done.5) | data formatting | bytes 36992 | tf_op jit(solution)/shard_map/ppermute | solution.py:19
  96.7 8.7 %pad_maximum_fusion.20 = (f32[3,32,32,256]{3,2,1,0:T(8,128)S(1)}, f32[3,32,32,256]{3,2,1,0:T(8,128)}) fusion(f32[4,34,34,1]{3,2,1,0:T(8,128)S(1)} %copy.33, f32[4,34,1,256]{3,2,1,0:T(1,128)S(1)} %collective-permute-done.2, f32[4,34,32,256]{3,2,1,0:T(8,128)} %copy-done, f32[4,34,1,256]{3,2,1,0:T(1,128)S(1)} %collective-permute-done.3, f32[4,34,34,1]{3,2,1,0:T(8,128)} %copy.35), kind=kLoop, calls=%fused_computation.63 | loop fusion | flops 4718592 | bytes 11063424 | tf_op jit(solution)/shard_map/concatenate | solution.py:21
  105.4 4.7 %fusion.87 = f32[32,32,256]{2,1,0:T(8,128)S(1)} fusion(f32[32,32,256]{2,1,0:T(8,128)S(1)} %copy-done.10, f32[32,6,256]{2,1,0:T(8,128)} %collective-permute-done.9, f32[32,6,256]{2,1,0:T(8,128)} %collective-permute-done.8), kind=kLoop, calls=%fused_computation.224 | loop fusion | flops 9699328 | bytes 2490368 | tf_op jit(solution)/shard_map/add | solution.py:28
  110.3 3.0 %collective-permute-start.10 = (f32[32,32,6]{2,1,0:T(8,128)S(1)}, f32[32,32,6]{2,1,0:T(8,128)S(1)}, u32[]{:S(2)}, u32[]{:S(2)}) collective-permute-start(f32[32,32,6]{2,1,0:T(8,128)S(1)} %get-tuple-element.37), channel_id=1, source_target_pairs={{0,1},{1,2},{2,3},{3,4},{4,5},{5,6},{6,7},{8,9},{9,10},{10,11},{11... | collective-permute-start | bytes 73736 | tf_op jit(solution)/shard_map/ppermute | solution.py:19
  116.0 8.9 %collective-permute-done.10 = f32[32,32,6]{2,1,0:T(8,128)S(1)} collective-permute-done((f32[32,32,6]{2,1,0:T(8,128)S(1)}, f32[32,32,6]{2,1,0:T(8,128)S(1)}, u32[]{:S(2)}, u32[]{:S(2)}) %collective-permute-start.10) | collective-permute-done | bytes 24608 | tf_op jit(solution)/shard_map/ppermute | solution.py:19
  124.9 5.6 %collective-permute-done.11 = f32[32,32,6]{2,1,0:T(8,128)S(1)} collective-permute-done((f32[32,32,6]{2,1,0:T(8,128)S(1)}, f32[32,32,6]{2,1,0:T(8,128)S(1)}, u32[]{:S(2)}, u32[]{:S(2)}) %collective-permute-start.11) | collective-permute-done | bytes 24608 | tf_op jit(solution)/shard_map/ppermute | solution.py:20
  130.5 5.4 %multiply_select_fusion = (f32[32,32,256]{2,1,0:T(8,128)S(1)}, f32[32,32,256]{2,1,0:T(8,128)S(1)}) fusion(f32[32,32,256]{2,1,0:T(8,128)S(1)} %copy-done.13, f32[32,32,256]{2,1,0:T(8,128)S(1)} %copy-done.12, s32[32,32,256]{2,1,0:T(8,128)S(1)} %copy-done.9, f32[32,32,6]{2,1,0:T(8,128)S(1)} %collective-permute-done.11, f32[32,32,256]{2,1,0:T(8,128)S(1)} %fusion.87, ...), kind=kLoop, calls=%fused_computation.389 | loop fusion | flops 14417920 | bytes 6340608 | tf_op jit(solution)/shard_map/jit(_where)/select_n | solution.py:76
  135.9 1.9 collective-permute-start.18
  137.8 5.7 %collective-permute-start.19 = (f32[6,32,256]{2,1,0:T(8,128)S(1)}, f32[6,32,256]{2,1,0:T(8,128)S(1)}, u32[]{:S(2)}, u32[]{:S(2)}) collective-permute-start(f32[6,32,256]{2,1,0:T(8,128)S(1)} %get-tuple-element.36), channel_id=1, source_target_pairs={{32,0},{64,32},{96,64},{128,96},{160,128},{192,160},{224,192},{33,... | collective-permute-start | bytes 589832 | tf_op jit(solution)/shard_map/ppermute | solution.py:20
  143.6 6.3 %fusion.209 = (f32[1,32,32,256]{3,2,1,0:T(8,128)}, f32[1,32,32,256]{3,2,1,0:T(8,128)}, f32[1,32,32,256]{3,2,1,0:T(8,128)}, f32[1,32,32,256]{3,2,1,0:T(8,128)}, f...) fusion(f32[34,34,258]{2,1,0:T(8,128)S(1)} %fusion.19, f32[3,32,32,256]{3,2,1,0:T(8,128)} %get-tuple-element.13, ...), kind=kLoop, calls=%fused_computation.356 | loop fusion | flops 8388608 | bytes 27017216 | tf_op jit(solution)/shard_map/stack | solution.py:67
  149.9 1.9 fusion.23
  152.7 3.2 %collective-permute-start.20 = (f32[32,6,256]{2,1,0:T(8,128)}, f32[32,6,256]{2,1,0:T(8,128)}, u32[]{:S(2)}, u32[]{:S(2)}) collective-permute-start(f32[32,6,256]{2,1,0:T(8,128)} %get-tuple-element.33), channel_id=1, source_target_pairs={{0,8},{8,16},{16,24},{1,9},{9,17},{17,25},{2,10},{10,18},{18,26},{... | collective-permute-start | bytes 589832 | tf_op jit(solution)/shard_map/ppermute | solution.py:19
  155.8 1.9 collective-permute-start.21
  157.8 18.4 %fusion.10 = f32[3,32,32,256]{3,2,1,0:T(8,128)} fusion(f32[4,34,1,256]{3,2,1,0:T(1,128)S(1)} %collective-permute-done.2, f32[4,34,1,256]{3,2,1,0:T(1,128)S(1)} %collective-permute-done.3, f32[4,1,32,256]{3,2,1,0:T(8,128)S(1)} %copy-done.16, f32[4,1,32,256]{3,2,1,0:T(8,128)S(1)} %collective-permute-done.1, f32[3,34,34,1]{3,2,1,0:T(8,128)} %copy.41, ...), kind=kLoop, calls=%fused_computation.41 | loop fusion | flops 35389440 | bytes 33479776 | tf_op jit(solution)/shard_map/jit(_where)/select_n | solution.py:69
  176.3 4.4 %fusion.55 = f32[32,32,256]{2,1,0:T(8,128)S(1)} fusion(f32[32,32,256]{2,1,0:T(8,128)S(1)} %fusion.23, f32[32,6,256]{2,1,0:T(8,128)} %collective-permute-done.21, f32[32,6,256]{2,1,0:T(8,128)} %collective-permute-done.20), kind=kLoop, calls=%fused_computation.192 | loop fusion | flops 9699328 | bytes 2490368 | tf_op jit(solution)/shard_map/add | solution.py:28
  180.9 4.9 %collective-permute-start.22 = (f32[32,32,6]{2,1,0:T(8,128)S(1)}, f32[32,32,6]{2,1,0:T(8,128)S(1)}, u32[]{:S(2)}, u32[]{:S(2)}) collective-permute-start(f32[32,32,6]{2,1,0:T(8,128)S(1)} %get-tuple-element.31), channel_id=1, source_target_pairs={{0,1},{1,2},{2,3},{3,4},{4,5},{5,6},{6,7},{8,9},{9,10},{10,11},{11... | collective-permute-start | bytes 73736 | tf_op jit(solution)/shard_map/ppermute | solution.py:19
  187.1 2.4 %pad_maximum_fusion.5 = f32[4,32,32,256]{3,2,1,0:T(8,128)} fusion(f32[1,32,32,256]{3,2,1,0:T(8,128)S(1)} %copy-done.14, f32[3,32,32,256]{3,2,1,0:T(8,128)S(1)} %copy-done.8), kind=kLoop, calls=%fused_computation.9 | loop fusion | flops 1048576 | bytes 8388608 | tf_op jit(solution)/shard_map/concatenate | solution.py:72
  189.5 7.5 %collective-permute-done.22 = f32[32,32,6]{2,1,0:T(8,128)S(1)} collective-permute-done((f32[32,32,6]{2,1,0:T(8,128)S(1)}, f32[32,32,6]{2,1,0:T(8,128)S(1)}, u32[]{:S(2)}, u32[]{:S(2)}) %collective-permute-start.22) | collective-permute-done | bytes 24608 | tf_op jit(solution)/shard_map/ppermute | solution.py:19
  197.0 4.2 %collective-permute-done.23 = f32[32,32,6]{2,1,0:T(8,128)S(1)} collective-permute-done((f32[32,32,6]{2,1,0:T(8,128)S(1)}, f32[32,32,6]{2,1,0:T(8,128)S(1)}, u32[]{:S(2)}, u32[]{:S(2)}) %collective-permute-start.23) | collective-permute-done | bytes 24608 | tf_op jit(solution)/shard_map/ppermute | solution.py:20
  201.1 6.1 %fusion.119 = f32[32,32,256]{2,1,0:T(8,128)} fusion(f32[32,32,256]{2,1,0:T(8,128)S(1)} %fusion.55, f32[32,32,6]{2,1,0:T(8,128)S(1)} %collective-permute-done.23, f32[32,32,6]{2,1,0:T(8,128)S(1)} %collective-permute-done.22), kind=kLoop, calls=%fused_computation.256 | loop fusion | flops 9699328 | bytes 2146304 | tf_op jit(solution)/shard_map/add | solution.py:28
  (90 shorter events, 14.1 us)
Async XLA Ops:
  0.6 25.4 %copy-start.6 = (f32[3,32,32,256]{3,2,1,0:T(8,128)S(1)}, f32[3,32,32,256]{3,2,1,0:T(8,128)}, u32[]{:S(2)}) copy-start(f32[3,32,32,256]{3,2,1,0:T(8,128)} %param.6) | copy-start | bytes 9437188
  1.9 42.2 %collective-permute-start.6 = (f32[6,32,256]{2,1,0:T(8,128)S(1)}, f32[6,32,256]{2,1,0:T(8,128)S(1)}, u32[]{:S(2)}, u32[]{:S(2)}) collective-permute-start(f32[6,32,256]{2,1,0:T(8,128)S(1)} %get-tuple-element.43), channel_id=1, source_target_pairs={{0,32},{32,64},{64,96},{96,128},{128,160},{160,192},{192,224},{1,3... | collective-permute-start | bytes 589832 | tf_op jit(solution)/shard_map/ppermute | solution.py:19
  5.0 44.5 %collective-permute-start.7 = (f32[6,32,256]{2,1,0:T(8,128)S(1)}, f32[6,32,256]{2,1,0:T(8,128)S(1)}, u32[]{:S(2)}, u32[]{:S(2)}) collective-permute-start(f32[6,32,256]{2,1,0:T(8,128)S(1)} %get-tuple-element.44), channel_id=1, source_target_pairs={{32,0},{64,32},{96,64},{128,96},{160,128},{192,160},{224,192},{33,... | collective-permute-start | bytes 589832 | tf_op jit(solution)/shard_map/ppermute | solution.py:20
  10.2 12.4 %collective-permute-start.13 = (f32[3,1,32,256]{3,2,1,0:T(8,128)S(1)}, f32[3,1,32,256]{3,2,1,0:T(8,128)S(1)}, u32[]{:S(2)}, u32[]{:S(2)}) collective-permute-start(f32[3,1,32,256]{3,2,1,0:T(8,128)S(1)} %get-tuple-element.24), channel_id=1, source_target_pairs={{0,32},{32,64},{64,96},{96,128},{128,160},{160,192},{192,224},{1,3... | collective-permute-start | bytes 294920 | tf_op jit(solution)/shard_map/ppermute | solution.py:19
  13.2 22.0 %collective-permute-start.1 = (f32[4,1,32,256]{3,2,1,0:T(8,128)S(1)}, f32[4,1,32,256]{3,2,1,0:T(8,128)S(1)}, u32[]{:S(2)}, u32[]{:S(2)}) collective-permute-start(f32[4,1,32,256]{3,2,1,0:T(8,128)S(1)} %get-tuple-element.17), channel_id=1, source_target_pairs={{0,32},{32,64},{64,96},{96,128},{128,160},{160,192},{192,224},{1,3... | collective-permute-start | bytes 393224 | tf_op jit(solution)/shard_map/ppermute | solution.py:19
  15.4 24.4 %collective-permute-start = (f32[4,1,32,256]{3,2,1,0:T(8,128)S(1)}, f32[4,1,32,256]{3,2,1,0:T(8,128)S(1)}, u32[]{:S(2)}, u32[]{:S(2)}) collective-permute-start(f32[4,1,32,256]{3,2,1,0:T(8,128)S(1)} %get-tuple-element.16), channel_id=1, source_target_pairs={{32,0},{64,32},{96,64},{128,96},{160,128},{192,160},{224,192},{33,... | collective-permute-start | bytes 393224 | tf_op jit(solution)/shard_map/ppermute | solution.py:20
  22.6 8.0 %collective-permute-start.12 = (f32[3,1,32,256]{3,2,1,0:T(8,128)S(1)}, f32[3,1,32,256]{3,2,1,0:T(8,128)S(1)}, u32[]{:S(2)}, u32[]{:S(2)}) collective-permute-start(f32[3,1,32,256]{3,2,1,0:T(8,128)S(1)} %get-tuple-element.23), channel_id=1, source_target_pairs={{32,0},{64,32},{96,64},{128,96},{160,128},{192,160},{224,192},{33,... | collective-permute-start | bytes 294920 | tf_op jit(solution)/shard_map/ppermute | solution.py:20
  26.0 13.0 %copy-start.1 = (f32[4,32,32,256]{3,2,1,0:T(8,128)S(1)}, f32[4,32,32,256]{3,2,1,0:T(8,128)}, u32[]{:S(2)}) copy-start(f32[4,32,32,256]{3,2,1,0:T(8,128)} %param.7) | copy-start | bytes 12582916
  30.7 9.1 %copy-start.20 = (f32[3,1,32,256]{3,2,1,0:T(8,128)}, f32[3,1,32,256]{3,2,1,0:T(8,128)S(1)}, u32[]{:S(2)}) copy-start(f32[3,1,32,256]{3,2,1,0:T(8,128)S(1)} %collective-permute-done.12) | copy-start | bytes 294916
  30.7 20.7 %copy-start.4 = (f32[3,34,32,256]{3,2,1,0:T(8,128)}, f32[3,34,32,256]{3,2,1,0:T(8,128)S(1)}, u32[]{:S(2)}) copy-start(f32[3,34,32,256]{3,2,1,0:T(8,128)S(1)} %constant_dynamic-update-slice_fusion.7) | copy-start | bytes 10027012
  30.9 20.6 %collective-permute-start.14 = (f32[3,34,1,256]{3,2,1,0:T(1,128)S(1)}, f32[3,34,1,256]{3,2,1,0:T(1,128)S(1)}, u32[]{:S(2)}, u32[]{:S(2)}) collective-permute-start(f32[3,34,1,256]{3,2,1,0:T(1,128)S(1)} %get-tuple-element.21), channel_id=1, source_target_pairs={{8,0},{16,8},{24,16},{9,1},{17,9},{25,17},{10,2},{18,10},{26,18},{... | collective-permute-start | bytes 313352 | tf_op jit(solution)/shard_map/ppermute | solution.py:20
  35.1 16.3 %collective-permute-start.15 = (f32[3,34,1,256]{3,2,1,0:T(1,128)S(1)}, f32[3,34,1,256]{3,2,1,0:T(1,128)S(1)}, u32[]{:S(2)}, u32[]{:S(2)}) collective-permute-start(f32[3,34,1,256]{3,2,1,0:T(1,128)S(1)} %get-tuple-element.20), channel_id=1, source_target_pairs={{0,8},{8,16},{16,24},{1,9},{9,17},{17,25},{2,10},{10,18},{18,26},{... | collective-permute-start | bytes 313352 | tf_op jit(solution)/shard_map/ppermute | solution.py:19
  39.0 10.2 %copy-start.11 = (f32[32,32,256]{2,1,0:T(8,128)S(1)}, f32[32,32,256]{2,1,0:T(8,128)}, u32[]{:S(2)}) copy-start(f32[32,32,256]{2,1,0:T(8,128)} %param.4) | copy-start | bytes 3145732
  39.8 9.4 %copy-start.15 = (f32[4,1,32,256]{3,2,1,0:T(8,128)}, f32[4,1,32,256]{3,2,1,0:T(8,128)S(1)}, u32[]{:S(2)}) copy-start(f32[4,1,32,256]{3,2,1,0:T(8,128)S(1)} %collective-permute-done) | copy-start | bytes 393220
  39.8 2.1 %copy-start = (f32[4,34,32,256]{3,2,1,0:T(8,128)}, f32[4,34,32,256]{3,2,1,0:T(8,128)S(1)}, u32[]{:S(2)}) copy-start(f32[4,34,32,256]{3,2,1,0:T(8,128)S(1)} %constant_dynamic-update-slice_fusion) | copy-start | bytes 13369348
  42.1 21.4 %collective-permute-start.2 = (f32[4,34,1,256]{3,2,1,0:T(1,128)S(1)}, f32[4,34,1,256]{3,2,1,0:T(1,128)S(1)}, u32[]{:S(2)}, u32[]{:S(2)}) collective-permute-start(f32[4,34,1,256]{3,2,1,0:T(1,128)S(1)} %get-tuple-element.15), channel_id=1, source_target_pairs={{8,0},{16,8},{24,16},{9,1},{17,9},{25,17},{10,2},{18,10},{26,18},{... | collective-permute-start | bytes 417800 | tf_op jit(solution)/shard_map/ppermute | solution.py:20
  44.0 19.5 %collective-permute-start.3 = (f32[4,34,1,256]{3,2,1,0:T(1,128)S(1)}, f32[4,34,1,256]{3,2,1,0:T(1,128)S(1)}, u32[]{:S(2)}, u32[]{:S(2)}) collective-permute-start(f32[4,34,1,256]{3,2,1,0:T(1,128)S(1)} %get-tuple-element.14), channel_id=1, source_target_pairs={{0,8},{8,16},{16,24},{1,9},{9,17},{17,25},{2,10},{10,18},{18,26},{... | collective-permute-start | bytes 417800 | tf_op jit(solution)/shard_map/ppermute | solution.py:19
  51.4 0.8 copy-start.17
  51.4 0.8 copy-start.19
  57.2 27.0 %collective-permute-start.16 = (f32[3,34,34,1]{2,3,1,0:T(1,128)}, f32[3,34,34,1]{2,3,1,0:T(1,128)S(1)}, u32[]{:S(2)}, u32[]{:S(2)}) collective-permute-start(f32[3,34,34,1]{2,3,1,0:T(1,128)} %copy.38), channel_id=1, source_target_pairs={{1,0},{2,1},{3,2},{4,3},{5,4},{6,5},{7,6},{9,8},{10,9},{11,10},{12... | collective-permute-start | bytes 41624 | tf_op jit(solution)/shard_map/ppermute | solution.py:20
  59.3 29.6 %collective-permute-start.17 = (f32[3,34,34,1]{2,3,1,0:T(1,128)S(1)}, f32[3,34,34,1]{2,3,1,0:T(1,128)S(1)}, u32[]{:S(2)}, u32[]{:S(2)}) collective-permute-start(f32[3,34,34,1]{2,3,1,0:T(1,128)S(1)} %copy.40), channel_id=1, source_target_pairs={{0,1},{1,2},{2,3},{3,4},{4,5},{5,6},{6,7},{8,9},{9,10},{10,11},{11... | collective-permute-start | bytes 41624 | tf_op jit(solution)/shard_map/ppermute | solution.py:19
  71.9 19.3 %collective-permute-start.4 = (f32[4,34,34,1]{2,0,3,1:T(4,128)S(1)}, f32[4,34,34,1]{2,0,3,1:T(4,128)}, u32[]{:S(2)}, u32[]{:S(2)}) collective-permute-start(f32[4,34,34,1]{2,0,3,1:T(4,128)S(1)} %copy.32), channel_id=1, source_target_pairs={{1,0},{2,1},{3,2},{4,3},{5,4},{6,5},{7,6},{9,8},{10,9},{11,10},{12... | collective-permute-start | bytes 55496 | tf_op jit(solution)/shard_map/ppermute | solution.py:20
  74.8 18.2 %collective-permute-start.5 = (f32[4,34,34,1]{2,0,3,1:T(4,128)}, f32[4,34,34,1]{2,0,3,1:T(4,128)}, u32[]{:S(2)}, u32[]{:S(2)}) collective-permute-start(f32[4,34,34,1]{2,0,3,1:T(4,128)} %copy.34), channel_id=1, source_target_pairs={{0,1},{1,2},{2,3},{3,4},{4,5},{5,6},{6,7},{8,9},{9,10},{10,11},{11... | collective-permute-start | bytes 55496 | tf_op jit(solution)/shard_map/ppermute | solution.py:19
  81.5 23.9 %collective-permute-start.8 = (f32[32,6,256]{2,1,0:T(8,128)}, f32[32,6,256]{2,1,0:T(8,128)}, u32[]{:S(2)}, u32[]{:S(2)}) collective-permute-start(f32[32,6,256]{2,1,0:T(8,128)} %get-tuple-element.39), channel_id=1, source_target_pairs={{0,8},{8,16},{16,24},{1,9},{9,17},{17,25},{2,10},{10,18},{18,26},{... | collective-permute-start | bytes 589832 | tf_op jit(solution)/shard_map/ppermute | solution.py:19
  84.2 21.2 %collective-permute-start.9 = (f32[32,6,256]{2,1,0:T(8,128)}, f32[32,6,256]{2,1,0:T(8,128)}, u32[]{:S(2)}, u32[]{:S(2)}) collective-permute-start(f32[32,6,256]{2,1,0:T(8,128)} %get-tuple-element.40), channel_id=1, source_target_pairs={{8,0},{16,8},{24,16},{9,1},{17,9},{25,17},{10,2},{18,10},{26,18},{... | collective-permute-start | bytes 589832 | tf_op jit(solution)/shard_map/ppermute | solution.py:20
  93.1 21.8 %slice-start = ((s8[4456448]{0:T(1024)(128)(4,1)}), s8[262144]{0:T(1024)(128)(4,1)S(1)}, s32[]{:S(2)}) async-start(s8[4456448]{0:T(1024)(128)(4,1)} %bitcast.16), calls=%async_computation | async-start | bytes 524288
  96.7 8.7 %copy-start.10 = (f32[32,32,256]{2,1,0:T(8,128)S(1)}, f32[32,32,256]{2,1,0:T(8,128)}, u32[]{:S(2)}) copy-start(f32[32,32,256]{2,1,0:T(8,128)} %fusion.214) | copy-start | bytes 3145732
  96.7 18.2 %slice-start.1 = ((s8[4456448]{0:T(1024)(128)(4,1)}), s8[4194304]{0:T(1024)(128)(4,1)S(1)}, s32[]{:S(2)}) async-start(s8[4456448]{0:T(1024)(128)(4,1)} %bitcast.16), calls=%async_computation.1 | async-start | bytes 8388608
  105.4 9.5 %copy-start.3 = (f32[4,34,34,1]{3,2,1,0:T(8,128)S(1)}, f32[4,34,34,1]{3,2,1,0:T(8,128)}, u32[]{:S(2)}) copy-start(f32[4,34,34,1]{3,2,1,0:T(8,128)} %copy.35) | copy-start | bytes 55492
  110.3 14.6 %collective-permute-start.10 = (f32[32,32,6]{2,1,0:T(8,128)S(1)}, f32[32,32,6]{2,1,0:T(8,128)S(1)}, u32[]{:S(2)}, u32[]{:S(2)}) collective-permute-start(f32[32,32,6]{2,1,0:T(8,128)S(1)} %get-tuple-element.37), channel_id=1, source_target_pairs={{0,1},{1,2},{2,3},{3,4},{4,5},{5,6},{6,7},{8,9},{9,10},{10,11},{11... | collective-permute-start | bytes 73736 | tf_op jit(solution)/shard_map/ppermute | solution.py:19
  113.3 17.2 %copy-start.9 = (s32[32,32,256]{2,1,0:T(8,128)S(1)}, s32[32,32,256]{2,1,0:T(8,128)}, u32[]{:S(2)}) copy-start(s32[32,32,256]{2,1,0:T(8,128)} %param.5) | copy-start | bytes 3145732
  113.3 17.2 %copy-start.12 = (f32[32,32,256]{2,1,0:T(8,128)S(1)}, f32[32,32,256]{2,1,0:T(8,128)}, u32[]{:S(2)}) copy-start(f32[32,32,256]{2,1,0:T(8,128)} %get-tuple-element.4) | copy-start | bytes 3145732
  113.3 17.2 %copy-start.13 = (f32[32,32,256]{2,1,0:T(8,128)S(1)}, f32[32,32,256]{2,1,0:T(8,128)}, u32[]{:S(2)}) copy-start(f32[32,32,256]{2,1,0:T(8,128)} %get-tuple-element.5) | copy-start | bytes 3145732
  113.3 17.1 %collective-permute-start.11 = (f32[32,32,6]{2,1,0:T(8,128)S(1)}, f32[32,32,6]{2,1,0:T(8,128)S(1)}, u32[]{:S(2)}, u32[]{:S(2)}) collective-permute-start(f32[32,32,6]{2,1,0:T(8,128)S(1)} %get-tuple-element.38), channel_id=1, source_target_pairs={{1,0},{2,1},{3,2},{4,3},{5,4},{6,5},{7,6},{9,8},{10,9},{11,10},{12... | collective-permute-start | bytes 73736 | tf_op jit(solution)/shard_map/ppermute | solution.py:20
  130.5 13.1 %copy-start.2 = (f32[4,32,32,256]{3,2,1,0:T(8,128)S(1)}, f32[4,32,32,256]{3,2,1,0:T(8,128)}, u32[]{:S(2)}) copy-start(f32[4,32,32,256]{3,2,1,0:T(8,128)} %param.7) | copy-start | bytes 12582916
  130.5 13.0 %copy-start.16 = (f32[4,1,32,256]{3,2,1,0:T(8,128)S(1)}, f32[4,1,32,256]{3,2,1,0:T(8,128)}, u32[]{:S(2)}) copy-start(f32[4,1,32,256]{3,2,1,0:T(8,128)} %copy-done.15) | copy-start | bytes 393220
  135.9 14.0 %collective-permute-start.18 = (f32[6,32,256]{2,1,0:T(8,128)S(1)}, f32[6,32,256]{2,1,0:T(8,128)S(1)}, u32[]{:S(2)}, u32[]{:S(2)}) collective-permute-start(f32[6,32,256]{2,1,0:T(8,128)S(1)} %get-tuple-element.35), channel_id=1, source_target_pairs={{0,32},{32,64},{64,96},{96,128},{128,160},{160,192},{192,224},{1,3... | collective-permute-start | bytes 589832 | tf_op jit(solution)/shard_map/ppermute | solution.py:19
  137.8 12.1 %collective-permute-start.19 = (f32[6,32,256]{2,1,0:T(8,128)S(1)}, f32[6,32,256]{2,1,0:T(8,128)S(1)}, u32[]{:S(2)}, u32[]{:S(2)}) collective-permute-start(f32[6,32,256]{2,1,0:T(8,128)S(1)} %get-tuple-element.36), channel_id=1, source_target_pairs={{32,0},{64,32},{96,64},{128,96},{160,128},{192,160},{224,192},{33,... | collective-permute-start | bytes 589832 | tf_op jit(solution)/shard_map/ppermute | solution.py:20
  143.6 14.2 %copy-start.7 = (f32[3,32,32,256]{3,2,1,0:T(8,128)S(1)}, f32[3,32,32,256]{3,2,1,0:T(8,128)}, u32[]{:S(2)}) copy-start(f32[3,32,32,256]{3,2,1,0:T(8,128)} %param.6) | copy-start | bytes 9437188
  149.9 7.9 %copy-start.5 = (f32[3,34,32,256]{3,2,1,0:T(8,128)S(1)}, f32[3,34,32,256]{3,2,1,0:T(8,128)}, u32[]{:S(2)}) copy-start(f32[3,34,32,256]{3,2,1,0:T(8,128)} %copy-done.4) | copy-start | bytes 10027012
  149.9 7.9 %copy-start.18 = (f32[3,34,1,256]{3,2,1,0:T(1,128)S(1)}, f32[3,34,1,256]{3,2,1,0:T(1,128)}, u32[]{:S(2)}) copy-start(f32[3,34,1,256]{3,2,1,0:T(1,128)} %copy-done.17) | copy-start | bytes 313348
  152.7 23.6 %collective-permute-start.20 = (f32[32,6,256]{2,1,0:T(8,128)}, f32[32,6,256]{2,1,0:T(8,128)}, u32[]{:S(2)}, u32[]{:S(2)}) collective-permute-start(f32[32,6,256]{2,1,0:T(8,128)} %get-tuple-element.33), channel_id=1, source_target_pairs={{0,8},{8,16},{16,24},{1,9},{9,17},{17,25},{2,10},{10,18},{18,26},{... | collective-permute-start | bytes 589832 | tf_op jit(solution)/shard_map/ppermute | solution.py:19
  155.8 20.4 %collective-permute-start.21 = (f32[32,6,256]{2,1,0:T(8,128)}, f32[32,6,256]{2,1,0:T(8,128)}, u32[]{:S(2)}, u32[]{:S(2)}) collective-permute-start(f32[32,6,256]{2,1,0:T(8,128)} %get-tuple-element.34), channel_id=1, source_target_pairs={{8,0},{16,8},{24,16},{9,1},{17,9},{25,17},{10,2},{18,10},{26,18},{... | collective-permute-start | bytes 589832 | tf_op jit(solution)/shard_map/ppermute | solution.py:20
  176.2 10.9 %copy-start.8 = (f32[3,32,32,256]{3,2,1,0:T(8,128)S(1)}, f32[3,32,32,256]{3,2,1,0:T(8,128)}, u32[]{:S(2)}) copy-start(f32[3,32,32,256]{3,2,1,0:T(8,128)} %fusion.10) | copy-start | bytes 9437188
  176.2 10.9 %copy-start.14 = (f32[1,32,32,256]{3,2,1,0:T(8,128)S(1)}, f32[1,32,32,256]{3,2,1,0:T(8,128)}, u32[]{:S(2)}) copy-start(f32[1,32,32,256]{3,2,1,0:T(8,128)} %get-tuple-element.28) | copy-start | bytes 3145732
  180.9 16.1 %collective-permute-start.22 = (f32[32,32,6]{2,1,0:T(8,128)S(1)}, f32[32,32,6]{2,1,0:T(8,128)S(1)}, u32[]{:S(2)}, u32[]{:S(2)}) collective-permute-start(f32[32,32,6]{2,1,0:T(8,128)S(1)} %get-tuple-element.31), channel_id=1, source_target_pairs={{0,1},{1,2},{2,3},{3,4},{4,5},{5,6},{6,7},{8,9},{9,10},{10,11},{11... | collective-permute-start | bytes 73736 | tf_op jit(solution)/shard_map/ppermute | solution.py:19
  185.8 15.4 %collective-permute-start.23 = (f32[32,32,6]{2,1,0:T(8,128)S(1)}, f32[32,32,6]{2,1,0:T(8,128)S(1)}, u32[]{:S(2)}, u32[]{:S(2)}) collective-permute-start(f32[32,32,6]{2,1,0:T(8,128)S(1)} %get-tuple-element.32), channel_id=1, source_target_pairs={{1,0},{2,1},{3,2},{4,3},{5,4},{6,5},{7,6},{9,8},{10,9},{11,10},{12... | collective-permute-start | bytes 73736 | tf_op jit(solution)/shard_map/ppermute | solution.py:20
where the time goes:
time: 208 us; the launch traced here: 207 us
  starting transfers between devices  75.3 us (36%)
  other arithmetic  71.7 us (34%)
  local copies, waits for them, and re-layouts  32.6 us (16%)
  waiting for transfers between devices  26.2 us (13%)
    ppermute x12, starting transfers between devices, extended(): before = lax.ppermute(last, axis, up)  40.8 us
    ppermute x12, starting transfers between devices, extended(): after = lax.ppermute(first, axis, down)  34.6 us
    add x5, other arithmetic, smooth_axis(): total + taps_list[k] * lax.slice_in_dim(field, k, k + count, axis=dim)  18.9 us
    select_n x1, other arithmetic, design_terms(): momentum = jnp.where(inlet, lam_c, momentum)  18.4 us
    ppermute x12, waiting for transfers between devices, extended(): before = lax.ppermute(last, axis, up)  16.4 us
    concatenate x3, other arithmetic, extended(): value = jnp.concatenate([before, value, after], axis=dim)  12.5 us
    slice x6, local copies, waits for them, and re-layouts, extended(): first = lax.slice_in_dim(value, 0, width, axis=dim)  12.2 us
    ppermute x12, waiting for transfers between devices, extended(): after = lax.ppermute(first, axis, down)  9.79 us
  transfers between devices with their start and end apart: 24, of which 4 were waited for; matrix products, arithmetic and copies ran while one was open for 37% of the time, Pallas kernels for 0%

commit v1 on v0

v1 whole, which is shorter than its diff:
```python
import math

import jax
import jax.numpy as jnp
from jax import lax
from jax.experimental import pallas as pl
from jax.experimental.pallas import tpu as pltpu
from jax.sharding import PartitionSpec as P

MESH = pl.DeviceIdType.MESH
NB = {"gx": 8, "gy": 4, "gz": 8}
X, Y, Z = 32, 32, 256
TANH2 = math.tanh(2.0)
CUBE = 1.0 / (49.0**3)

NAMES = (
    [f"a{c}{i}" for c in "yz" for i in (0, 1)]
    + [f"ad{i}{j}" for i in (0, 1) for j in (0, 1)]
    + [f"{c}{i}" for c in ("e", "bn", "bf", "fx", "fy", "fz", "dy", "dz") for i in (0, 1)]
    + [f"dd{i}{j}" for i in (0, 1) for j in (0, 1)]
)
SLOT = {n: i for i, n in enumerate(NAMES)}


def exists(offs):
    ok = None
    for axis, d in offs.items():
        i = lax.axis_index(axis)
        c = (i > 0) if d < 0 else (i < NB[axis] - 1)
        ok = c if ok is None else jnp.logical_and(ok, c)
    return ok


class Msg:
    def __init__(self, sems, name, offs, src, dst):
        self.offs = offs
        self.back = {a: -d for a, d in offs.items()}
        k = SLOT[name]
        self.copy = pltpu.make_async_remote_copy(
            src_ref=src,
            dst_ref=dst,
            send_sem=sems[0].at[k],
            recv_sem=sems[1].at[k],
            device_id={a: lax.axis_index(a) + d for a, d in offs.items()},
            device_id_type=MESH,
        )

    def start(self):
        @pl.when(exists(self.offs))
        def _():
            self.copy.start()

    def wait_recv(self):
        @pl.when(exists(self.back))
        def _():
            self.copy.wait_recv()

    def wait_send(self):
        @pl.when(exists(self.offs))
        def _():
            self.copy.wait_send()


def enter():
    barrier = pltpu.get_barrier_semaphore()
    total = jnp.int32(0)
    offs = [{a: d} for a in NB for d in (-1, 1)]
    offs += [{"gy": i, "gz": j} for i in (-1, 1) for j in (-1, 1)]
    for o in offs:
        c = exists(o)

        @pl.when(c)
        def _():
            pl.semaphore_signal(
                barrier, inc=1, device_id={a: lax.axis_index(a) + d for a, d in o.items()}, device_id_type=MESH
            )

        total = total + c.astype(jnp.int32)
    return barrier, total


def lanes(shape):
    return lax.broadcasted_iota(jnp.int32, shape, len(shape) - 1)


def rows(shape):
    return lax.broadcasted_iota(jnp.int32, shape, len(shape) - 2)


def y_filter(ref, *at):
    acc = 7.0 * ref[(*at, pl.ds(8, Y))]
    for k in range(1, 7):
        acc = acc + (7.0 - k) * (ref[(*at, pl.ds(8 - k, Y))] + ref[(*at, pl.ds(8 + k, Y))])
    return acc


def x_filter(ref, at):
    acc = 7.0 * ref[at + 6]
    for k in range(1, 7):
        acc = acc + (7.0 - k) * (ref[at + 6 - k] + ref[at + 6 + k])
    return acc


def split(v):
    hi = v.astype(jnp.bfloat16)
    lo = (v - hi.astype(jnp.float32)).astype(jnp.bfloat16)
    return jnp.concatenate([hi, lo], axis=0)


def pack_z(ref, first, out):
    slot = lanes((Y, 128)) // 8

    def pair(j, carry):
        left = jnp.zeros((Y, 128), jnp.float32)
        right = jnp.zeros((Y, 128), jnp.float32)
        for s in range(16):
            x = j * 16 + s
            a = ref[x, pl.ds(first, Y), 0:128]
            b = ref[x, pl.ds(first, Y), 128:256]
            a = a if s == 0 else pltpu.roll(a, 8 * s, 1)
            b = b if s == 15 else pltpu.roll(b, 8 * s + 8, 1)
            left = jnp.where(slot == s, a, left)
            right = jnp.where(slot == s, b, right)
        out[0, j] = left
        out[1, j] = right
        return carry

    lax.fori_loop(0, 2, pair, 0)


def y_strips(zx, zy):
    for side in (0, 1):
        for j in (0, 1):
            zy[side, j] = y_filter(zx, side, j)


def yz_group(ref, zy, band, edge, x0, put):
    lane = lanes((Y, 128))
    body = [y_filter(ref, x0 + i) for i in range(4)]
    ends = []
    for i in range(4):
        x = x0 + i
        s, j = x % 16, x // 16
        before = pltpu.roll(zy[0, j], 120 - 8 * s, 1)
        after = pltpu.roll(zy[1, j], 128 - 8 * s, 1)
        ends.append(jnp.where(lane < 64, after, before))
    full = split(jnp.concatenate(body, axis=0))
    tips = split(jnp.concatenate(ends, axis=0))
    res = jnp.dot(full, band[...], preferred_element_type=jnp.float32)
    res = res + jnp.dot(tips, edge[...], preferred_element_type=jnp.float32)
    res = res[: 4 * Y] + res[4 * Y :]
    for i in range(4):
        put(x0 + i, res[i * Y : (i + 1) * Y])


def y_up(v):
    return jnp.where(rows(v.shape) == Y - 1, 0.0, pltpu.roll(v, Y - 1, 0))


def y_dn(v):
    return jnp.where(rows(v.shape) == 0, 0.0, pltpu.roll(v, 1, 0))


def z_up(v):
    return jnp.where(lanes(v.shape) == Z - 1, 0.0, pltpu.roll(v, Z - 1, 1))


def z_dn(v):
    return jnp.where(lanes(v.shape) == 0, 0.0, pltpu.roll(v, 1, 1))


def kernel(
    den_h, kind_h, vel_h, adj_h, res_o, sen_o,
    den, kind, vel, adj, zp, zx, zy, zp2, zx2, filt, em, pw, alpha, grid, res, sen,
    cxs, cxr, cys, cyr, czs, czr, band, edge, send, recv, load,
):
    sems = (send, recv)
    ix, iy, iz = (lax.axis_index(a) for a in NB)
    loads = [
        pltpu.make_async_copy(den_h, den.at[:, pl.ds(8, Y), :], load.at[0]),
        pltpu.make_async_copy(vel_h, vel, load.at[1]),
        pltpu.make_async_copy(adj_h, adj, load.at[2]),
        pltpu.make_async_copy(kind_h, kind, load.at[3]),
    ]
    for c in loads:
        c.start()
    barrier, total = enter()

    @pl.when(ix == 0)
    def _():
        filt[0:12] = jnp.zeros((12, Y, Z), jnp.float32)
        em[0:6] = jnp.zeros((6, Y, Z), jnp.float32)
        cxr[0] = jnp.zeros((4, Y, Z), jnp.float32)

    @pl.when(ix == NB["gx"] - 1)
    def _():
        filt[44:56] = jnp.zeros((12, Y, Z), jnp.float32)
        em[38:44] = jnp.zeros((6, Y, Z), jnp.float32)
        cxr[1] = jnp.zeros((4, Y, Z), jnp.float32)

    @pl.when(iz == 0)
    def _():
        zx[0] = jnp.zeros((2, 48, 128), jnp.float32)
        zx2[0] = jnp.zeros((2, 48, 128), jnp.float32)
        czr[0] = jnp.zeros((Y, 128), jnp.float32)

    @pl.when(iz == NB["gz"] - 1)
    def _():
        zx[1] = jnp.zeros((2, 48, 128), jnp.float32)
        zx2[1] = jnp.zeros((2, 48, 128), jnp.float32)
        czr[1] = jnp.zeros((Y, 128), jnp.float32)

    for edge_at, first in ((0, 0), (NB["gy"] - 1, 40)):

        @pl.when(iy == edge_at)
        def _():
            for r in (zx, zx2):
                r[:, :, pl.ds(first, 8), :] = jnp.zeros((2, 2, 8, 128), jnp.float32)
            for r in (den, grid):
                r[:, pl.ds(first, 8), :] = jnp.zeros((X, 8, Z), jnp.float32)

    def clear(x, carry):
        for side in (0, 1):
            for c in range(4):
                cyr[side, c, x] = jnp.zeros((8, Z), jnp.float32)
        return carry

    lax.fori_loop(0, X, clear, 0)

    i, j = rows((Z, Z)), lanes((Z, Z))
    band[...] = jnp.maximum(7 - jnp.abs(i - j), 0).astype(jnp.float32).astype(jnp.bfloat16)
    i, j = rows((128, Z)), lanes((128, Z))
    i = jnp.where(i < 64, i + Z, i - 128)
    edge[...] = jnp.maximum(7 - jnp.abs(i - j), 0).astype(jnp.float32).astype(jnp.bfloat16)

    loads[0].wait()
    pack_z(den, 8, zp)
    pl.semaphore_wait(barrier, total)

    def yz_messages(name, src, packed, dst, strips, first):
        out = [
            Msg(sems, f"{name}y0", {"gy": -1}, src.at[:, pl.ds(first, 6), :], dst.at[:, pl.ds(40, 6), :]),
            Msg(sems, f"{name}y1", {"gy": 1}, src.at[:, pl.ds(first + 26, 6), :], dst.at[:, pl.ds(2, 6), :]),
            Msg(sems, f"{name}z0", {"gz": -1}, packed.at[0], strips.at[1, :, pl.ds(8, Y), :]),
            Msg(sems, f"{name}z1", {"gz": 1}, packed.at[1], strips.at[0, :, pl.ds(8, Y), :]),
        ]
        for a, (d, mine, there) in enumerate(((-1, 0, 40), (1, 26, 2))):
            for b, e in enumerate((-1, 1)):
                out.append(
                    Msg(
                        sems, f"{name}d{a}{b}", {"gy": d, "gz": e},
                        packed.at[b, :, pl.ds(mine, 6), :], strips.at[1 - b, :, pl.ds(there, 6), :],
                    )
                )
        return out

    msg_a = yz_messages("a", den, zp, den, zx, 8)
    for m in msg_a:
        m.start()

    for c in loads[1:]:
        c.wait()

    def energy(x, carry):
        e = None
        for d in range(3):
            u = vel[d, x]
            t = u * (u + adj[d, x])
            e = t if e is None else e + t
        em[x + 6] = jnp.where(kind[x] == 0, e, 0.0)
        return carry

    lax.fori_loop(0, X, energy, 0)
    msg_e = [
        Msg(sems, "e0", {"gx": -1}, em.at[6:12], em.at[38:44]),
        Msg(sems, "e1", {"gx": 1}, em.at[32:38], em.at[0:6]),
    ]
    for m in msg_e:
        m.start()

    lane = lanes((Y, 128))

    def stencil(x, carry, lower, upper):
        to_prev, to_next = carry
        lam = [adj[d, x] for d in range(3)]
        mu2 = adj[3, x] * 0.5
        w = [lam[d] + 2.0 * vel[d, x] for d in range(3)]
        plus = [w[d] + mu2 for d in range(3)]
        minus = [w[d] - mu2 for d in range(3)]

        def at(d, q):
            return adj[d, q] + 2.0 * vel[d, q]

        out = []
        for d in range(3):
            t = y_up(plus[1] if d == 1 else w[d]) + y_dn(minus[1] if d == 1 else w[d])
            t = t + z_up(plus[2] if d == 2 else w[d]) + z_dn(minus[2] if d == 2 else w[d])
            if lower:
                t = t + at(d, x - 1)
                if d == 0:
                    t = t - 0.5 * adj[3, x - 1]
            if upper:
                t = t + at(d, x + 1)
                if d == 0:
                    t = t + 0.5 * adj[3, x + 1]
            out.append(-t)
        div = y_up(lam[1]) - y_dn(lam[1]) + z_up(lam[2]) - z_dn(lam[2])
        if upper:
            div = div + adj[0, x + 1]
        if lower:
            div = div - adj[0, x - 1]
        out.append(-0.5 * div)
        for c in range(4):
            res[c, x] = out[c]

        if not lower:
            cxs[0, 0], cxs[0, 1], cxs[0, 2], cxs[0, 3] = -plus[0], -w[1], -w[2], -0.5 * lam[0]
        if not upper:
            cxs[1, 0], cxs[1, 1], cxs[1, 2], cxs[1, 3] = -minus[0], -w[1], -w[2], 0.5 * lam[0]
        for side, part, end, sign in ((0, plus, slice(0, 8), -0.5), (1, minus, slice(Y - 8, Y), 0.5)):
            cys[side, 0, x] = -w[0][end]
            cys[side, 1, x] = -part[1][end]
            cys[side, 2, x] = -w[2][end]
            cys[side, 3, x] = sign * lam[1][end]
        zs0 = (-w[0], -w[1], -plus[2], -0.5 * lam[2])
        zs1 = (-w[0], -w[1], -minus[2], 0.5 * lam[2])
        for c in range(4):
            at_lane = c * X + x
            first = pltpu.roll(zs0[c][:, 0:128], at_lane, 1)
            last = pltpu.roll(zs1[c][:, 128:256], lax.rem(at_lane + 1, 128), 1)
            to_prev = jnp.where(lane == at_lane, first, to_prev)
            to_next = jnp.where(lane == at_lane, last, to_next)
        return to_prev, to_next

    ends = (jnp.zeros((Y, 128), jnp.float32), jnp.zeros((Y, 128), jnp.float32))
    ends = stencil(0, ends, False, True)
    ends = lax.fori_loop(1, X - 1, lambda x, c: stencil(x, c, True, True), ends)
    ends = stencil(X - 1, ends, True, False)
    czs[0], czs[1] = ends

    msg_f = [
        Msg(sems, "fx0", {"gx": -1}, cxs.at[0], cxr.at[1]),
        Msg(sems, "fx1", {"gx": 1}, cxs.at[1], cxr.at[0]),
        Msg(sems, "fy0", {"gy": -1}, cys.at[0, :, :, 0:1, :], cyr.at[1, :, :, 7:8, :]),
        Msg(sems, "fy1", {"gy": 1}, cys.at[1, :, :, 7:8, :], cyr.at[0, :, :, 0:1, :]),
        Msg(sems, "fz0", {"gz": -1}, czs.at[0], czr.at[1]),
        Msg(sems, "fz1", {"gz": 1}, czs.at[1], czr.at[0]),
    ]

    for m in msg_a:
        m.wait_recv()
    y_strips(zx, zy)

    def put_filt(x, v):
        filt[x + 12] = v

    def outer(g, carry):
        yz_group(den, zy, band, edge, g * 4, put_filt)
        yz_group(den, zy, band, edge, 20 + g * 4, put_filt)
        return carry

    lax.fori_loop(0, 3, outer, 0)
    msg_b = [
        Msg(sems, "bn0", {"gx": -1}, filt.at[12:18], filt.at[44:50]),
        Msg(sems, "bn1", {"gx": 1}, filt.at[38:44], filt.at[6:12]),
        Msg(sems, "bf0", {"gx": -1}, filt.at[18:24], filt.at[50:56]),
        Msg(sems, "bf1", {"gx": 1}, filt.at[32:38], filt.at[0:6]),
    ]
    for m in msg_b:
        m.start()
    for m in msg_f:
        m.start()
    for g in (12, 16):
        yz_group(den, zy, band, edge, g, put_filt)

    def project(e):
        t = jnp.tanh(x_filter(filt, e) * (4.0 * CUBE) - 2.0)
        r = 1.0 / (1.0 + (TANH2 + t) * (0.5 / TANH2))
        pw[e] = (-8.0 / TANH2) * (r * r) * (1.0 - t * t) * em[e]
        return r

    def project_own(x, carry):
        r = project(x + 6)
        k = kind[x]
        alpha[x] = jnp.where(k == 0, 4.0 * r - 2.0, jnp.where(k == 1, 2.0, 0.0))
        return carry

    def project_halo(e, carry):
        project(e)
        return carry

    def smooth_x(x, carry):
        grid[x, pl.ds(8, Y), :] = x_filter(pw, x)
        return carry

    lax.fori_loop(6, 26, project_own, 0)
    for m in msg_b[:2]:
        m.wait_recv()
    for lo, hi in ((0, 6), (26, 32)):
        lax.fori_loop(lo, hi, project_own, 0)
    lax.fori_loop(6, 26, smooth_x, 0)
    for m in msg_e:
        m.wait_recv()
    for m in msg_b[2:]:
        m.wait_recv()
    for lo, hi in ((0, 6), (38, 44)):
        lax.fori_loop(lo, hi, project_halo, 0)
    for lo, hi in ((0, 6), (26, 32)):
        lax.fori_loop(lo, hi, smooth_x, 0)

    pack_z(grid, 8, zp2)
    msg_d = yz_messages("d", grid, zp2, grid, zx2, 8)
    for m in msg_d:
        m.start()

    for m in msg_f:
        m.wait_recv()
    for c in range(4):
        res[c, 0] += cxr[0, c]
        res[c, X - 1] += cxr[1, c]

    def finish(x, carry):
        a = alpha[x] + 6.0
        k = kind[x]
        for c in range(4):
            at_lane = c * X + x
            first = pltpu.roll(czr[0], lax.rem(128 - at_lane, 128), 1)
            last = pltpu.roll(czr[1], 127 - at_lane, 1)
            res[c, x, 0:8] += cyr[0, c, x]
            res[c, x, Y - 8 : Y] += cyr[1, c, x]
            r = res[c, x] + jnp.concatenate([jnp.where(lane == 0, first, 0.0), jnp.where(lane == 127, last, 0.0)], axis=1)
            v = adj[c, x]
            if c < 3:
                res[c, x] = jnp.where(k == 2, v, r + a * (v + 2.0 * vel[c, x]))
            else:
                res[c, x] = jnp.where(k == 3, v, r)
        return carry

    lax.fori_loop(0, X, finish, 0)
    out_r = pltpu.make_async_copy(res, res_o, load.at[4])
    out_r.start()

    for m in msg_d:
        m.wait_recv()
    y_strips(zx2, zy)

    def put_sen(x, v):
        sen[x] = v * CUBE

    def last(g, carry):
        yz_group(grid, zy, band, edge, g * 4, put_sen)
        return carry

    lax.fori_loop(0, 8, last, 0)
    out_s = pltpu.make_async_copy(sen, sen_o, load.at[5])
    out_s.start()
    for m in msg_a + msg_e + msg_b + msg_f + msg_d:
        m.wait_send()
    out_r.wait()
    out_s.wait()


def body(density, voxel_kind, velocity, adjoint):
    f32 = jnp.float32
    block = (X, Y, Z)
    strips, wide = (2, 2, Y, 128), (2, 2, 48, 128)
    return pl.pallas_call(
        kernel,
        out_shape=(jax.ShapeDtypeStruct((4, *block), f32), jax.ShapeDtypeStruct(block, f32)),
        in_specs=[pl.BlockSpec(memory_space=pl.ANY)] * 4,
        out_specs=(pl.BlockSpec(memory_space=pl.ANY),) * 2,
        scratch_shapes=[
            pltpu.VMEM((X, 48, Z), f32),
            pltpu.VMEM(block, jnp.int32),
            pltpu.VMEM((3, *block), f32),
            pltpu.VMEM((4, *block), f32),
            pltpu.VMEM(strips, f32),
            pltpu.VMEM(wide, f32),
            pltpu.VMEM(strips, f32),
            pltpu.VMEM(strips, f32),
            pltpu.VMEM(wide, f32),
            pltpu.VMEM((56, Y, Z), f32),
            pltpu.VMEM((44, Y, Z), f32),
            pltpu.VMEM((44, Y, Z), f32),
            pltpu.VMEM(block, f32),
            pltpu.VMEM((X, 48, Z), f32),
            pltpu.VMEM((4, *block), f32),
            pltpu.VMEM(block, f32),
            pltpu.VMEM((2, 4, Y, Z), f32),
            pltpu.VMEM((2, 4, Y, Z), f32),
            pltpu.VMEM((2, 4, X, 8, Z), f32),
            pltpu.VMEM((2, 4, X, 8, Z), f32),
            pltpu.VMEM((2, Y, 128), f32),
            pltpu.VMEM((2, Y, 128), f32),
            pltpu.VMEM((Z, Z), jnp.bfloat16),
            pltpu.VMEM((128, Z), jnp.bfloat16),
            pltpu.SemaphoreType.DMA((len(NAMES),)),
            pltpu.SemaphoreType.DMA((len(NAMES),)),
            pltpu.SemaphoreType.DMA((6,)),
        ],
        compiler_params=pltpu.CompilerParams(
            collective_id=0, has_side_effects=True, vmem_limit_bytes=44 * 2**20
        ),
    )(density, voxel_kind, velocity, adjoint)


def solution(mesh):
    own = P("gx", "gy", "gz")
    fields = P(None, "gx", "gy", "gz")
    return jax.shard_map(
        body, mesh=mesh, in_specs=(own, own, fields, fields), out_specs=(fields, own), check_vma=False
    )
```

time: 208 us -> 48.9 us (0.24)
  the two profiles are of different devices: /device:TPU:9 before, /device:TPU:97 now
where the time goes in v1:
time: 48.9 us; the launch traced here: 48.6 us
  Pallas kernels  37.9 us (78%)
  local copies, waits for them, and re-layouts  10.1 us (21%)
  between operations  0.65 us (1%)
    pallas_call x1, Pallas kernels, body(): pl.pallas_call(kernel, out_shape=(jax.ShapeDtypeStruct((4, *block), f32),...  37.9 us
    unnamed x8, local copies, waits for them, and re-layouts  10.1 us

profile of v1, /device:TPU:97, one launch (start us, length us, event | category | flops | bytes accessed | tf_op | source)
XLA Modules:
  0.0 48.6 jit_solution(16612428789710629279)
XLA Ops:
  0.6 0.0 copy-start
  0.6 1.9 %copy-done = f32[3,32,32,256]{3,2,1,0:T(8,128)S(1)} copy-done((f32[3,32,32,256]{3,2,1,0:T(8,128)S(1)}, f32[3,32,32,256]{3,2,1,0:T(8,128)}, u32[]{:S(2)}) %copy-start) | copy-done | bytes 3145752
  2.5 0.0 copy-start.1
  2.5 1.2 %copy-done.1 = f32[32,32,256]{2,1,0:T(8,128)S(1)} copy-done((f32[32,32,256]{2,1,0:T(8,128)S(1)}, f32[32,32,256]{2,1,0:T(8,128)}, u32[]{:S(2)}) %copy-start.1) | copy-done | bytes 1048600
  3.7 0.0 copy-start.2
  3.7 1.2 %copy-done.2 = s32[32,32,256]{2,1,0:T(8,128)S(1)} copy-done((s32[32,32,256]{2,1,0:T(8,128)S(1)}, s32[32,32,256]{2,1,0:T(8,128)}, u32[]{:S(2)}) %copy-start.2) | copy-done | bytes 1048600
  5.0 37.9 %shard_map.59 = (f32[4,32,32,256]{3,2,1,0:T(8,128)}, f32[32,32,256]{2,1,0:T(8,128)S(1)}) custom-call(f32[32,32,256]{2,1,0:T(8,128)S(1)} %copy-done.1, s32[32,32,256]{2,1,0:T(8,128)S(1)} %copy-done.2, f32[3,32,32,256]{3,2,1,0:T(8,128)S(1)} %copy-done, f32[4,32,32,256]{3,2,1,0:T(8,128)} %adj_h.1), custom_call_target="tpu_custom_call" | custom-call | tf_op jit(solution)/shard_map/pallas_call | solution.py:467
  42.9 4.8 %copy.8 = f32[4,32,32,256]{3,2,1,0:T(8,128)} copy(f32[4,32,32,256]{3,2,1,0:T(8,128)} %get-tuple-element.4) | data formatting | bytes 8388608
  47.7 1.0 %copy.9 = f32[32,32,256]{2,1,0:T(8,128)} copy(f32[32,32,256]{2,1,0:T(8,128)S(1)} %get-tuple-element.5) | data formatting | bytes 2097152
Async XLA Ops:
  0.6 1.9 %copy-start = (f32[3,32,32,256]{3,2,1,0:T(8,128)S(1)}, f32[3,32,32,256]{3,2,1,0:T(8,128)}, u32[]{:S(2)}) copy-start(f32[3,32,32,256]{3,2,1,0:T(8,128)} %vel_h.1) | copy-start | bytes 9437188
  2.5 1.2 %copy-start.1 = (f32[32,32,256]{2,1,0:T(8,128)S(1)}, f32[32,32,256]{2,1,0:T(8,128)}, u32[]{:S(2)}) copy-start(f32[32,32,256]{2,1,0:T(8,128)} %den_h.1) | copy-start | bytes 3145732
  3.7 1.2 %copy-start.2 = (s32[32,32,256]{2,1,0:T(8,128)S(1)}, s32[32,32,256]{2,1,0:T(8,128)}, u32[]{:S(2)}) copy-start(s32[32,32,256]{2,1,0:T(8,128)} %kind_h.1) | copy-start | bytes 3145732

commit v2 on v1

--- a/solution.py
+++ b/solution.py
@@ -170,9 +170,9 @@
 
 
 def kernel(
-    den_h, kind_h, vel_h, adj_h, res_o, sen_o,
-    den, kind, vel, adj, zp, zx, zy, zp2, zx2, filt, em, pw, alpha, grid, res, sen,
-    cxs, cxr, cys, cyr, czs, czr, band, edge, send, recv, load,
+    den_h, kind_h, vel_h, adj_h, res, grid, zx2, band, edge,
+    den, kind, vel, adj, zp, zx, zy, zp2, filt, em, pw, alpha,
+    cxs, cxr, cys, cyr, czs, czr, send, recv, load,
 ):
     sems = (send, recv)
     ix, iy, iz = (lax.axis_index(a) for a in NB)
@@ -437,11 +437,16 @@
         return carry
 
     lax.fori_loop(0, X, finish, 0)
-    out_r = pltpu.make_async_copy(res, res_o, load.at[4])
-    out_r.start()
 
     for m in msg_d:
         m.wait_recv()
+    for m in msg_a + msg_e + msg_b + msg_f + msg_d:
+        m.wait_send()
+
+
+def finish_kernel(res, grid, zx2, band, edge, res_o, sen_o, zy, sen, sems):
+    out_r = pltpu.make_async_copy(res, res_o, sems.at[0])
+    out_r.start()
     y_strips(zx2, zy)
 
     def put_sen(x, v):
@@ -452,23 +457,28 @@
         return carry
 
     lax.fori_loop(0, 8, last, 0)
-    out_s = pltpu.make_async_copy(sen, sen_o, load.at[5])
+    out_s = pltpu.make_async_copy(sen, sen_o, sems.at[1])
     out_s.start()
-    for m in msg_a + msg_e + msg_b + msg_f + msg_d:
-        m.wait_send()
     out_r.wait()
     out_s.wait()
 
 
-def body(density, voxel_kind, velocity, adjoint):
+def body(*args):
     f32 = jnp.float32
     block = (X, Y, Z)
     strips, wide = (2, 2, Y, 128), (2, 2, 48, 128)
-    return pl.pallas_call(
+    vmem = pl.BlockSpec(memory_space=pltpu.VMEM)
+    near = pl.pallas_call(
         kernel,
-        out_shape=(jax.ShapeDtypeStruct((4, *block), f32), jax.ShapeDtypeStruct(block, f32)),
+        out_shape=(
+            pltpu.VMEM((4, *block), f32),
+            pltpu.VMEM((X, 48, Z), f32),
+            pltpu.VMEM(wide, f32),
+            pltpu.VMEM((Z, Z), jnp.bfloat16),
+            pltpu.VMEM((128, Z), jnp.bfloat16),
+        ),
         in_specs=[pl.BlockSpec(memory_space=pl.ANY)] * 4,
-        out_specs=(pl.BlockSpec(memory_space=pl.ANY),) * 2,
+        out_specs=(vmem,) * 5,
         scratch_shapes=[
             pltpu.VMEM((X, 48, Z), f32),
             pltpu.VMEM(block, jnp.int32),
@@ -478,13 +488,9 @@
             pltpu.VMEM(wide, f32),
             pltpu.VMEM(strips, f32),
             pltpu.VMEM(strips, f32),
-            pltpu.VMEM(wide, f32),
             pltpu.VMEM((56, Y, Z), f32),
             pltpu.VMEM((44, Y, Z), f32),
             pltpu.VMEM((44, Y, Z), f32),
-            pltpu.VMEM(block, f32),
-            pltpu.VMEM((X, 48, Z), f32),
-            pltpu.VMEM((4, *block), f32),
             pltpu.VMEM(block, f32),
             pltpu.VMEM((2, 4, Y, Z), f32),
             pltpu.VMEM((2, 4, Y, Z), f32),
@@ -492,16 +498,26 @@
             pltpu.VMEM((2, 4, X, 8, Z), f32),
             pltpu.VMEM((2, Y, 128), f32),
             pltpu.VMEM((2, Y, 128), f32),
-            pltpu.VMEM((Z, Z), jnp.bfloat16),
-            pltpu.VMEM((128, Z), jnp.bfloat16),
             pltpu.SemaphoreType.DMA((len(NAMES),)),
             pltpu.SemaphoreType.DMA((len(NAMES),)),
-            pltpu.SemaphoreType.DMA((6,)),
+            pltpu.SemaphoreType.DMA((4,)),
         ],
         compiler_params=pltpu.CompilerParams(
-            collective_id=0, has_side_effects=True, vmem_limit_bytes=44 * 2**20
+            collective_id=0, has_side_effects=True, vmem_limit_bytes=32 * 2**20
         ),
-    )(density, voxel_kind, velocity, adjoint)
+    )(*(pltpu.with_memory_space_constraint(a, pltpu.HBM) for a in args))
+    return pl.pallas_call(
+        finish_kernel,
+        out_shape=(jax.ShapeDtypeStruct((4, *block), f32), jax.ShapeDtypeStruct(block, f32)),
+        in_specs=[vmem] * 5,
+        out_specs=(pl.BlockSpec(memory_space=pl.ANY),) * 2,
+        scratch_shapes=[
+            pltpu.VMEM(strips, f32),
+            pltpu.VMEM(block, f32),
+            pltpu.SemaphoreType.DMA((2,)),
+        ],
+        compiler_params=pltpu.CompilerParams(vmem_limit_bytes=16 * 2**20),
+    )(*near)
 
 
 def solution(mesh):

time: 48.9 us -> 39.6 us (0.81)
  local copies, waits for them, and re-layouts: 10.1 us -> 0 us
  Pallas kernels: 37.9 us -> 38.8 us
    unnamed x8 -> x0, local copies, waits for them, and re-layouts: 10.1 us -> none
    pallas_call x1 -> x2, Pallas kernels: 37.9 us -> 38.8 us  [the longest x1 34.7 us: body(): pl.pallas_call(kernel, out_shape=(pltpu.VMEM((4, *block), f32), pltpu.VME...]
where the time goes in v2:
time: 39.6 us; the launch traced here: 39.5 us
  Pallas kernels  38.8 us (98%)
  between operations  0.64 us (2%)
    pallas_call x1, Pallas kernels, body(): pl.pallas_call(kernel, out_shape=(pltpu.VMEM((4, *block), f32), pltpu.VME...  34.7 us
    pallas_call x1, Pallas kernels, body(): pl.pallas_call(finish_kernel, out_shape=(jax.ShapeDtypeStruct((4, *block)...  4.12 us

profile of v2, /device:TPU:97, one launch (start us, length us, event | category | flops | bytes accessed | tf_op | source)
XLA Modules:
  0.0 39.5 jit_solution(16340549140106347737)
XLA Ops:
  0.6 34.7 %shard_map.59 = (f32[4,32,32,256]{3,2,1,0:T(8,128)S(1)}, f32[32,48,256]{2,1,0:T(8,128)S(1)}, f32[2,2,48,128]{3,2,1,0:T(8,128)S(1)}, bf16[256,256]{1,0:T(8,128)(2,1)S(1)}, bf16[128,256]{1,0:T(8,128)(2,1)S(1)}) custom-call(f32[32,32,256]{2,1,0:T(8,128)} %den_h.1, s32[32,32,256]{2,1,0:T(8,128)} %kind_h.1, f32[3,32,32,256]{3,2,1,0:T(8,128)} %vel_h.1, ...), custom_call_target="tpu_custom_call" | custom-call | tf_op jit(solution)/shard_map/pallas_call | solution.py:471
  35.4 4.1 %shard_map.60 = (f32[4,32,32,256]{3,2,1,0:T(8,128)}, f32[32,32,256]{2,1,0:T(8,128)}) custom-call(f32[4,32,32,256]{3,2,1,0:T(8,128)S(1)} %get-tuple-element.7.res, f32[32,48,256]{2,1,0:T(8,128)S(1)} %get-tuple-element.8.grid, f32[2,2,48,128]{3,2,1,0:T(8,128)S(1)} %get-tuple-element.9.zx2, bf16[256,256]{1,0:T(8,128)(2,1)S(1)} %get-tuple-element.10.band, ...), custom_call_target="tpu_custom_call" | custom-call | tf_op jit(solution)/shard_map/pallas_call | solution.py:509

commit v3 on v2

v3 whole, which is shorter than its diff:
```python
import math

import jax
import jax.numpy as jnp
from jax import lax
from jax.experimental import pallas as pl
from jax.experimental.pallas import tpu as pltpu
from jax.sharding import PartitionSpec as P

MESH = pl.DeviceIdType.MESH
NB = {"gx": 8, "gy": 4, "gz": 8}
X, Y, Z = 32, 32, 256
TANH2 = math.tanh(2.0)
CUBE = 1.0 / (49.0**3)

NAMES = (
    [f"{k}y{i}{part}" for k in "ad" for i in (0, 1) for part in "lhm"]
    + [f"{k}z{i}" for k in "ad" for i in (0, 1)]
    + [f"{k}d{i}{j}" for k in "ad" for i in (0, 1) for j in (0, 1)]
    + [f"{c}{k}{i}" for c in "bc" for k in range(3) for i in (0, 1)]
    + [f"f{c}{i}" for c in "xyz" for i in (0, 1)]
)
PARTS = {"l": (0, 6), "h": (26, 32), "m": (6, 26)}
SLOT = {n: i for i, n in enumerate(NAMES)}


def exists(offs):
    ok = None
    for axis, d in offs.items():
        i = lax.axis_index(axis)
        c = (i > 0) if d < 0 else (i < NB[axis] - 1)
        ok = c if ok is None else jnp.logical_and(ok, c)
    return ok


class Msg:
    def __init__(self, sems, name, offs, src, dst):
        self.offs = offs
        self.back = {a: -d for a, d in offs.items()}
        k = SLOT[name]
        self.copy = pltpu.make_async_remote_copy(
            src_ref=src,
            dst_ref=dst,
            send_sem=sems[0].at[k],
            recv_sem=sems[1].at[k],
            device_id={a: lax.axis_index(a) + d for a, d in offs.items()},
            device_id_type=MESH,
        )

    def start(self):
        @pl.when(exists(self.offs))
        def _():
            self.copy.start()

    def wait_recv(self):
        @pl.when(exists(self.back))
        def _():
            self.copy.wait_recv()

    def wait_send(self):
        @pl.when(exists(self.offs))
        def _():
            self.copy.wait_send()


def enter():
    barrier = pltpu.get_barrier_semaphore()
    total = jnp.int32(0)
    offs = [{a: d} for a in NB for d in (-1, 1)]
    offs += [{"gy": i, "gz": j} for i in (-1, 1) for j in (-1, 1)]
    for o in offs:
        c = exists(o)

        @pl.when(c)
        def _():
            pl.semaphore_signal(
                barrier, inc=1, device_id={a: lax.axis_index(a) + d for a, d in o.items()}, device_id_type=MESH
            )

        total = total + c.astype(jnp.int32)
    return barrier, total


def lanes(shape):
    return lax.broadcasted_iota(jnp.int32, shape, len(shape) - 1)


def rows(shape):
    return lax.broadcasted_iota(jnp.int32, shape, len(shape) - 2)


def y_filter(ref, *at):
    acc = 7.0 * ref[(*at, pl.ds(8, Y))]
    for k in range(1, 7):
        acc = acc + (7.0 - k) * (ref[(*at, pl.ds(8 - k, Y))] + ref[(*at, pl.ds(8 + k, Y))])
    return acc


def y_local(v):
    def run(u):
        n = u.shape[0]
        two = u[: n - 1] + u[1:]
        three = two[: n - 2] + u[2:]
        four = three[: n - 3] + u[3:]
        return four[: n - 6] + three[4 : n - 2]

    zero = jnp.zeros((8, Z), jnp.float32)
    return run(run(jnp.concatenate([zero, v, zero], axis=0)[2:46]))


def x_run(ref, e, n, at):
    v = [ref[e + i, pl.ds(at, 8), :] for i in range(n + 12)]
    for _ in range(2):
        t = v[0]
        for u in v[1:7]:
            t = t + u
        out = [t]
        for i in range(7, len(v)):
            t = t + (v[i] - v[i - 7])
            out.append(t)
        v = out
    return v


def split(v):
    hi = v.astype(jnp.bfloat16)
    lo = (v - hi.astype(jnp.float32)).astype(jnp.bfloat16)
    return jnp.concatenate([hi, lo], axis=0)


def times(v, mat):
    n = v.shape[0]
    r = jnp.dot(split(v), mat[...], preferred_element_type=jnp.float32)
    return r[:n] + r[n:]


def fill_mats(band, tips):
    def put(ref, dist):
        ref[...] = jnp.maximum(7 - dist, 0).astype(jnp.float32).astype(jnp.bfloat16)

    i, j = rows((Z, Z)), lanes((Z, Z))
    put(band, jnp.abs(i - j))
    i, j = rows((128, 128)), lanes((128, 128))
    same = i // 8 == j // 8
    put(tips.at[0], jnp.where(same, 8 + j - i, 9))
    put(tips.at[1], jnp.where(same, 8 + i - j, 9))


def pack_z(ref, xs, out, fresh):
    slot = lanes((Y, 128)) // 8
    for j in (0, 1):
        left = jnp.zeros((Y, 128), jnp.float32) if fresh else out[0, j]
        right = jnp.zeros((Y, 128), jnp.float32) if fresh else out[1, j]
        for x in xs:
            if x // 16 != j:
                continue
            s = x % 16
            a = ref[x, :, 0:128]
            b = ref[x, :, 128:256]
            a = a if s == 0 else pltpu.roll(a, 8 * s, 1)
            b = b if s == 15 else pltpu.roll(b, 8 * s + 8, 1)
            left = jnp.where(slot == s, a, left)
            right = jnp.where(slot == s, b, right)
        out[0, j] = left
        out[1, j] = right


def yz_local(ref, band, x0, n, put):
    v = times(jnp.concatenate([y_local(ref[x0 + i]) for i in range(n)], axis=0), band)
    for i in range(n):
        put(x0 + i, v[i * Y : (i + 1) * Y])


def z_strips(strips, tips, zy):
    for side in (0, 1):
        v = jnp.concatenate([y_filter(strips, side, j) for j in (0, 1)], axis=0)
        v = times(v, tips.at[side])
        for j in (0, 1):
            zy[side, j] = v[j * Y : (j + 1) * Y]


def y_faces(faces, band, x0, n):
    out = []
    row = rows((n, 8, Z))
    for side in (0, 1):
        t = faces[side, x0 : x0 + n]
        acc = None
        for k in range(1, 7):
            if side == 0:
                u = jnp.where(row < k, (7.0 - k) * pltpu.roll(t, k, 1), 0.0)
            else:
                u = jnp.where(row >= 8 - k, (7.0 - k) * pltpu.roll(t, 8 - k, 1), 0.0)
            acc = u if acc is None else acc + u
        out.append(acc.reshape(n * 8, Z))
    v = times(jnp.concatenate(out, axis=0), band)
    return v[: n * 8].reshape(n, 8, Z), v[n * 8 :].reshape(n, 8, Z)


def yz_halo(faces, zy, band, x0, n, old, put):
    lane = lanes((Y, 128))
    first, last = y_faces(faces, band, x0, n)
    for i in range(n):
        x = x0 + i
        s, j = x % 16, x // 16
        lo, hi = zy[0, j], zy[1, j]
        lo = lo if s == 0 else pltpu.roll(lo, 128 - 8 * s, 1)
        hi = hi if s == 15 else pltpu.roll(hi, 120 - 8 * s, 1)
        v = old(x) + jnp.concatenate([jnp.where(lane < 8, lo, 0.0), jnp.where(lane >= 120, hi, 0.0)], axis=1)
        put(x, jnp.concatenate([v[0:8] + first[i], v[8 : Y - 8], v[Y - 8 : Y] + last[i]], axis=0))


def y_up(v):
    return jnp.where(rows(v.shape) == Y - 1, 0.0, pltpu.roll(v, Y - 1, 0))


def y_dn(v):
    return jnp.where(rows(v.shape) == 0, 0.0, pltpu.roll(v, 1, 0))


def z_up(v):
    return jnp.where(lanes(v.shape) == Z - 1, 0.0, pltpu.roll(v, Z - 1, 1))


def z_dn(v):
    return jnp.where(lanes(v.shape) == 0, 0.0, pltpu.roll(v, 1, 1))


def kernel(
    den_h, kind_h, vel_h, adj_h, res, sen, yf2, zx2, band, tips,
    den, kind, vel, adj, zp, yf, zx, zy, zp2, filt, em, pw, alpha, grid,
    cxs, cxr, cys, cyr, czs, czr, send, recv, load,
):
    sems = (send, recv)
    ix, iy, iz = (lax.axis_index(a) for a in NB)
    loads = [
        pltpu.make_async_copy(den_h, den, load.at[0]),
        pltpu.make_async_copy(vel_h, vel, load.at[1]),
        pltpu.make_async_copy(adj_h, adj, load.at[2]),
        pltpu.make_async_copy(kind_h, kind, load.at[3]),
    ]
    for c in loads:
        c.start()
    barrier, total = enter()

    f32 = jnp.float32

    @pl.when(ix == 0)
    def _():
        filt[0:6] = jnp.zeros((6, Y, Z), f32)
        pw[0:6] = jnp.zeros((6, Y, Z), f32)
        cxr[0] = jnp.zeros((4, Y, Z), f32)

    @pl.when(ix == NB["gx"] - 1)
    def _():
        filt[38:44] = jnp.zeros((6, Y, Z), f32)
        pw[38:44] = jnp.zeros((6, Y, Z), f32)
        cxr[1] = jnp.zeros((4, Y, Z), f32)

    for side, at in ((0, 0), (1, NB["gz"] - 1)):

        @pl.when(iz == at)
        def _():
            zx[side] = jnp.zeros((2, 48, 128), f32)
            zx2[side] = jnp.zeros((2, 48, 128), f32)
            czr[side] = jnp.zeros((Y, 128), f32)

    for side, at in ((0, 0), (1, NB["gy"] - 1)):

        @pl.when(iy == at)
        def _():
            for r in (zx, zx2):
                r[:, :, pl.ds(40 * side, 8), :] = jnp.zeros((2, 2, 8, 128), f32)
            for r in (yf, yf2):
                r[side] = jnp.zeros((X, 8, Z), f32)
            cyr[side] = jnp.zeros((4, X, Z), f32)

    fill_mats(band, tips)

    def face_messages(name, src, faces, parts):
        out = []
        for p in parts:
            lo, hi = PARTS[p]
            xs = pl.ds(lo, hi - lo)
            out += [
                Msg(sems, f"{name}y0{p}", {"gy": -1}, src.at[xs, 0:6, :], faces.at[1, xs, 0:6, :]),
                Msg(sems, f"{name}y1{p}", {"gy": 1}, src.at[xs, Y - 6 : Y, :], faces.at[0, xs, 2:8, :]),
            ]
        return out

    def strip_messages(name, packed, strips):
        out = [
            Msg(sems, f"{name}z0", {"gz": -1}, packed.at[0], strips.at[1, :, pl.ds(8, Y), :]),
            Msg(sems, f"{name}z1", {"gz": 1}, packed.at[1], strips.at[0, :, pl.ds(8, Y), :]),
        ]
        for a, (d, mine, there) in enumerate(((-1, 0, 40), (1, 26, 2))):
            for b, e in enumerate((-1, 1)):
                out.append(
                    Msg(
                        sems, f"{name}d{a}{b}", {"gy": d, "gz": e},
                        packed.at[b, :, pl.ds(mine, 6), :], strips.at[1 - b, :, pl.ds(there, 6), :],
                    )
                )
        return out

    loads[0].wait()
    pack_z(den, range(X), zp, True)
    pl.semaphore_wait(barrier, total)
    msg_an = face_messages("a", den, yf, "lh")
    msg_az = strip_messages("a", zp, zx)
    msg_am = face_messages("a", den, yf, "m")
    for m in msg_an + msg_az + msg_am:
        m.start()

    for c in loads[1:]:
        c.wait()

    for side, x, sign in ((0, 0, 0.5), (1, X - 1, -0.5)):
        w = [adj[d, x] + 2.0 * vel[d, x] for d in range(3)]
        cxs[side, 0] = -(w[0] + sign * adj[3, x])
        cxs[side, 1] = -w[1]
        cxs[side, 2] = -w[2]
        cxs[side, 3] = -sign * adj[0, x]
    msg_f = [
        Msg(sems, "fx0", {"gx": -1}, cxs.at[0], cxr.at[1]),
        Msg(sems, "fx1", {"gx": 1}, cxs.at[1], cxr.at[0]),
        Msg(sems, "fy0", {"gy": -1}, cys.at[0], cyr.at[1]),
        Msg(sems, "fy1", {"gy": 1}, cys.at[1], cyr.at[0]),
        Msg(sems, "fz0", {"gz": -1}, czs.at[0], czr.at[1]),
        Msg(sems, "fz1", {"gz": 1}, czs.at[1], czr.at[0]),
    ]

    for m in msg_f[:2]:
        m.start()

    def energy(x, carry):
        e = None
        for d in range(3):
            u = vel[d, x]
            t = u * (u + adj[d, x])
            e = t if e is None else e + t
        em[x] = jnp.where(kind[x] == 0, e, 0.0)
        return carry

    lax.fori_loop(0, X, energy, 0)

    def put_filt(x, v):
        filt[x + 6] = v

    def old_filt(x):
        return filt[x + 6]

    for x0, n in ((0, 6), (26, 6), (6, 10), (16, 10)):
        yz_local(den, band, x0, n, put_filt)

    lane = lanes((Y, 128))

    def stencil(x, carry, lower, upper):
        to_prev, to_next = carry
        lam = [adj[d, x] for d in range(3)]
        mu2 = adj[3, x] * 0.5
        w = [lam[d] + 2.0 * vel[d, x] for d in range(3)]
        plus = [w[d] + mu2 for d in range(3)]
        minus = [w[d] - mu2 for d in range(3)]

        def at(d, q):
            return adj[d, q] + 2.0 * vel[d, q]

        out = []
        for d in range(3):
            t = y_up(plus[1] if d == 1 else w[d]) + y_dn(minus[1] if d == 1 else w[d])
            t = t + z_up(plus[2] if d == 2 else w[d]) + z_dn(minus[2] if d == 2 else w[d])
            if lower:
                t = t + at(d, x - 1)
                if d == 0:
                    t = t - 0.5 * adj[3, x - 1]
            if upper:
                t = t + at(d, x + 1)
                if d == 0:
                    t = t + 0.5 * adj[3, x + 1]
            out.append(-t)
        div = y_up(lam[1]) - y_dn(lam[1]) + z_up(lam[2]) - z_dn(lam[2])
        if upper:
            div = div + adj[0, x + 1]
        if lower:
            div = div - adj[0, x - 1]
        out.append(-0.5 * div)
        for c in range(4):
            res[c, x] = out[c]

        for side, part, end, sign in ((0, plus, slice(0, 1), -0.5), (1, minus, slice(Y - 1, Y), 0.5)):
            cys[side, 0, pl.ds(x, 1)] = -w[0][end]
            cys[side, 1, pl.ds(x, 1)] = -part[1][end]
            cys[side, 2, pl.ds(x, 1)] = -w[2][end]
            cys[side, 3, pl.ds(x, 1)] = sign * lam[1][end]
        zs0 = (-w[0], -w[1], -plus[2], -0.5 * lam[2])
        zs1 = (-w[0], -w[1], -minus[2], 0.5 * lam[2])
        for c in range(4):
            at_lane = c * X + x
            first = pltpu.roll(zs0[c][:, 0:128], at_lane, 1)
            last = pltpu.roll(zs1[c][:, 128:256], lax.rem(at_lane + 1, 128), 1)
            to_prev = jnp.where(lane == at_lane, first, to_prev)
            to_next = jnp.where(lane == at_lane, last, to_next)
        return to_prev, to_next

    ends = (jnp.zeros((Y, 128), f32), jnp.zeros((Y, 128), f32))
    ends = stencil(0, ends, False, True)
    ends = lax.fori_loop(1, 12, lambda x, c: stencil(x, c, True, True), ends)

    for m in msg_an + msg_az:
        m.wait_recv()
    z_strips(zx, tips, zy)

    def x_messages(name, ref):
        out = []
        for k in range(3):
            out.append([
                Msg(sems, f"{name}{k}0", {"gx": -1}, ref.at[pl.ds(6 + 2 * k, 2)], ref.at[pl.ds(38 + 2 * k, 2)]),
                Msg(sems, f"{name}{k}1", {"gx": 1}, ref.at[pl.ds(36 - 2 * k, 2)], ref.at[pl.ds(4 - 2 * k, 2)]),
            ])
        return out

    msg_b = x_messages("b", filt)
    for x0 in (0, 26):
        yz_halo(yf, zy, band, x0, 6, old_filt, put_filt)
    for ms in msg_b:
        for m in ms:
            m.start()
    for m in msg_am:
        m.wait_recv()
    for x0 in (6, 16):
        yz_halo(yf, zy, band, x0, 10, old_filt, put_filt)

    def project(x, n):
        def strip(q, carry):
            at = pl.multiple_of(q * 8, 8)
            for i, f in enumerate(x_run(filt, x, n, at)):
                t = jnp.tanh(f * (4.0 * CUBE) - 2.0)
                r = 1.0 / (1.0 + (TANH2 + t) * (0.5 / TANH2))
                here = (x + i, pl.ds(at, 8))
                pw[x + i + 6, pl.ds(at, 8)] = (-8.0 / TANH2) * (r * r) * (1.0 - t * t) * em[here]
                k = kind[here]
                alpha[here] = jnp.where(k == 0, 4.0 * r - 2.0, jnp.where(k == 1, 2.0, 0.0))
            return carry

        lax.fori_loop(0, Y // 8, strip, 0)

    def smooth_x(x, n):
        def strip(q, carry):
            at = pl.multiple_of(q * 8, 8)
            for i, f in enumerate(x_run(pw, x, n, at)):
                grid[x + i, pl.ds(at, 8)] = f
            return carry

        lax.fori_loop(0, Y // 8, strip, 0)

    def put_sen(x, v):
        sen[x] = v

    for x in (6, 16):
        project(x, 10)

    ends = lax.fori_loop(12, X - 1, lambda x, c: stencil(x, c, True, True), ends)
    ends = stencil(X - 1, ends, True, False)
    czs[0], czs[1] = ends
    for m in msg_f[2:]:
        m.start()

    msg_c = x_messages("c", pw)
    for k in range(3):
        for m in msg_b[k]:
            m.wait_recv()
        for x in (4 - 2 * k, 26 + 2 * k):
            project(x, 2)
        for m in msg_c[2 - k]:
            m.start()

    for x in (6, 16):
        smooth_x(x, 10)
    msg_dm = face_messages("d", grid, yf2, "m")
    for m in msg_dm:
        m.start()
    pack_z(grid, range(6, 26), zp2, True)
    for x0 in (6, 16):
        yz_local(grid, band, x0, 10, put_sen)

    for m in msg_f[2:]:
        m.wait_recv()

    def finish(x, carry):
        a = alpha[x] + 6.0
        k = kind[x]
        row = rows((8, Z))
        for c in range(4):
            at_lane = c * X + x
            first = pltpu.roll(czr[0], (128 - at_lane) % 128, 1)
            last = pltpu.roll(czr[1], 127 - at_lane, 1)
            top = jnp.where(row == 0, cyr[0, c, pl.ds(x, 1)], 0.0)
            end = jnp.where(row == 7, cyr[1, c, pl.ds(x, 1)], 0.0)
            r = res[c, x]
            r = jnp.concatenate([r[0:8] + top, r[8 : Y - 8], r[Y - 8 : Y] + end], axis=0)
            r = r + jnp.concatenate([jnp.where(lane == 0, first, 0.0), jnp.where(lane == 127, last, 0.0)], axis=1)
            v = adj[c, x]
            if c < 3:
                res[c, x] = jnp.where(k == 2, v, r + a * (v + 2.0 * vel[c, x]))
            else:
                res[c, x] = jnp.where(k == 3, v, r)
        return carry

    lax.fori_loop(1, 12, finish, 0)
    for ms in msg_c:
        for m in ms:
            m.wait_recv()
    for x in (0, 26):
        smooth_x(x, 6)

    msg_dn = face_messages("d", grid, yf2, "lh")
    for m in msg_dn:
        m.start()
    pack_z(grid, (*range(0, 6), *range(26, 32)), zp2, False)
    msg_dz = strip_messages("d", zp2, zx2)
    for m in msg_dz:
        m.start()
    for x0 in (0, 26):
        yz_local(grid, band, x0, 6, put_sen)

    lax.fori_loop(12, X - 1, finish, 0)
    for m in msg_f[:2]:
        m.wait_recv()
    for side, x in ((0, 0), (1, X - 1)):
        for c in range(4):
            res[c, x] += cxr[side, c]
        finish(x, 0)

    for m in msg_dn + msg_dm + msg_dz:
        m.wait_recv()
    for m in msg_an + msg_am + msg_az + sum(msg_b + msg_c, []) + msg_f + msg_dn + msg_dm + msg_dz:
        m.wait_send()


def finish_kernel(res, sen_in, yf2, zx2, band, tips, res_o, sen_o, zy, sen, sems):
    out_r = pltpu.make_async_copy(res, res_o, sems.at[0])
    out_r.start()
    z_strips(zx2, tips, zy)

    def old(x):
        return sen_in[x]

    def put(x, v):
        sen[x] = v * CUBE

    out_s = []
    for g in range(2):
        yz_halo(yf2, zy, band, g * 16, 16, old, put)
        part = pl.ds(g * 16, 16)
        out_s.append(pltpu.make_async_copy(sen.at[part], sen_o.at[part], sems.at[1 + g]))
        out_s[-1].start()
    out_r.wait()
    for c in out_s:
        c.wait()


def body(*args):
    f32 = jnp.float32
    block = (X, Y, Z)
    strips, wide = (2, 2, Y, 128), (2, 2, 48, 128)
    vmem = pl.BlockSpec(memory_space=pltpu.VMEM)
    near = pl.pallas_call(
        kernel,
        out_shape=(
            pltpu.VMEM((4, *block), f32),
            pltpu.VMEM(block, f32),
            pltpu.VMEM((2, X, 8, Z), f32),
            pltpu.VMEM(wide, f32),
            pltpu.VMEM((Z, Z), jnp.bfloat16),
            pltpu.VMEM((2, 128, 128), jnp.bfloat16),
        ),
        in_specs=[pl.BlockSpec(memory_space=pl.ANY)] * 4,
        out_specs=(vmem,) * 6,
        scratch_shapes=[
            pltpu.VMEM(block, f32),
            pltpu.VMEM(block, jnp.int32),
            pltpu.VMEM((3, *block), f32),
            pltpu.VMEM((4, *block), f32),
            pltpu.VMEM(strips, f32),
            pltpu.VMEM((2, X, 8, Z), f32),
            pltpu.VMEM(wide, f32),
            pltpu.VMEM(strips, f32),
            pltpu.VMEM(strips, f32),
            pltpu.VMEM((44, Y, Z), f32),
            pltpu.VMEM(block, f32),
            pltpu.VMEM((44, Y, Z), f32),
            pltpu.VMEM(block, f32),
            pltpu.VMEM(block, f32),
            pltpu.VMEM((2, 4, Y, Z), f32),
            pltpu.VMEM((2, 4, Y, Z), f32),
            pltpu.VMEM((2, 4, X, Z), f32),
            pltpu.VMEM((2, 4, X, Z), f32),
            pltpu.VMEM((2, Y, 128), f32),
            pltpu.VMEM((2, Y, 128), f32),
            pltpu.SemaphoreType.DMA((len(NAMES),)),
            pltpu.SemaphoreType.DMA((len(NAMES),)),
            pltpu.SemaphoreType.DMA((4,)),
        ],
        compiler_params=pltpu.CompilerParams(
            collective_id=0, has_side_effects=True, vmem_limit_bytes=32 * 2**20
        ),
    )(*(pltpu.with_memory_space_constraint(a, pltpu.HBM) for a in args))
    return pl.pallas_call(
        finish_kernel,
        out_shape=(jax.ShapeDtypeStruct((4, *block), f32), jax.ShapeDtypeStruct(block, f32)),
        in_specs=[vmem] * 6,
        out_specs=(pl.BlockSpec(memory_space=pl.ANY),) * 2,
        scratch_shapes=[
            pltpu.VMEM(strips, f32),
            pltpu.VMEM(block, f32),
            pltpu.SemaphoreType.DMA((3,)),
        ],
        compiler_params=pltpu.CompilerParams(vmem_limit_bytes=16 * 2**20),
    )(*near)


def solution(mesh):
    own = P("gx", "gy", "gz")
    fields = P(None, "gx", "gy", "gz")
    return jax.shard_map(
        body, mesh=mesh, in_specs=(own, own, fields, fields), out_specs=(fields, own), check_vma=False
    )
```

time: 39.6 us -> 35.4 us (0.89)
  the two profiles are of different devices: /device:TPU:97 before, /device:TPU:77 now
where the time goes in v3:
time: 35.4 us; the launch traced here: 35.3 us
  Pallas kernels  34.7 us (98%)
  between operations  0.64 us (2%)
    pallas_call x1, Pallas kernels, body(): pl.pallas_call(kernel, out_shape=(pltpu.VMEM((4, *block), f32), pltpu.VME...  32.3 us
    pallas_call x1, Pallas kernels, body(): pl.pallas_call(finish_kernel, out_shape=(jax.ShapeDtypeStruct((4, *block)...  2.36 us

profile of v3, /device:TPU:77, one launch (start us, length us, event | category | flops | bytes accessed | tf_op | source)
XLA Modules:
  0.0 35.3 jit_solution(17820041283802635806)
XLA Ops:
  0.6 32.3 %shard_map.59 = (f32[4,32,32,256]{3,2,1,0:T(8,128)S(1)}, f32[32,32,256]{2,1,0:T(8,128)S(1)}, f32[2,32,8,256]{3,2,1,0:T(8,128)S(1)}, f32[2,2,48,128]{3,2,1,0:T(8,...) custom-call(f32[32,32,256]{2,1,0:T(8,128)} %den_h.1, s32[32,32,256]{2,1,0:T(8,128)} %kind_h.1, ...), custom_call_target="tpu_custom_call" | custom-call | tf_op jit(solution)/shard_map/pallas_call | solution.py:567
  33.0 2.4 %shard_map.60 = (f32[4,32,32,256]{3,2,1,0:T(8,128)}, f32[32,32,256]{2,1,0:T(8,128)}) custom-call(f32[4,32,32,256]{3,2,1,0:T(8,128)S(1)} %get-tuple-element.8.res, f32[32,32,256]{2,1,0:T(8,128)S(1)} %get-tuple-element.9.sen_in, f32[2,32,8,256]{3,2,1,0:T(8,128)S(1)} %get-tuple-element.10.yf2, f32[2,2,48,128]{3,2,1,0:T(8,128)S(1)} %get-tuple-element.11.zx2, ...), custom_call_target="tpu_custom_call" | custom-call | tf_op jit(solution)/shard_map/pallas_call | solution.py:608

commit v4 on v3

--- a/solution.py
+++ b/solution.py
@@ -238,9 +238,8 @@
         pltpu.make_async_copy(adj_h, adj, load.at[2]),
         pltpu.make_async_copy(kind_h, kind, load.at[3]),
     ]
-    for c in loads:
-        c.start()
     barrier, total = enter()
+    loads[0].start()
 
     f32 = jnp.float32
 
@@ -288,10 +287,7 @@
         return out
 
     def strip_messages(name, packed, strips):
-        out = [
-            Msg(sems, f"{name}z0", {"gz": -1}, packed.at[0], strips.at[1, :, pl.ds(8, Y), :]),
-            Msg(sems, f"{name}z1", {"gz": 1}, packed.at[1], strips.at[0, :, pl.ds(8, Y), :]),
-        ]
+        out = []
         for a, (d, mine, there) in enumerate(((-1, 0, 40), (1, 26, 2))):
             for b, e in enumerate((-1, 1)):
                 out.append(
@@ -300,17 +296,30 @@
                         packed.at[b, :, pl.ds(mine, 6), :], strips.at[1 - b, :, pl.ds(there, 6), :],
                     )
                 )
-        return out
+        return out + [
+            Msg(sems, f"{name}z0", {"gz": -1}, packed.at[0], strips.at[1, :, pl.ds(8, Y), :]),
+            Msg(sems, f"{name}z1", {"gz": 1}, packed.at[1], strips.at[0, :, pl.ds(8, Y), :]),
+        ]
 
     loads[0].wait()
+    for c in loads[1:]:
+        c.start()
     pack_z(den, range(X), zp, True)
     pl.semaphore_wait(barrier, total)
-    msg_an = face_messages("a", den, yf, "lh")
+    msg_an = face_messages("a", den_h, yf, "lh")
     msg_az = strip_messages("a", zp, zx)
-    msg_am = face_messages("a", den, yf, "m")
-    for m in msg_an + msg_az + msg_am:
+    msg_am = face_messages("a", den_h, yf, "m")
+    for m in msg_az + msg_an + msg_am:
         m.start()
 
+    def put_filt(x, v):
+        filt[x + 6] = v
+
+    def old_filt(x):
+        return filt[x + 6]
+
+    for x0, n in ((0, 6), (26, 6), (6, 10), (16, 10)):
+        yz_local(den, band, x0, n, put_filt)
     for c in loads[1:]:
         c.wait()
 
@@ -329,8 +338,16 @@
         Msg(sems, "fz1", {"gz": 1}, czs.at[1], czr.at[0]),
     ]
 
-    for m in msg_f[:2]:
-        m.start()
+
+    def y_ends(x, carry):
+        for side, part, at, sign in ((0, pl.ds(0, 8), 0, 0.5), (1, pl.ds(Y - 8, 8), 7, -0.5)):
+            w = [adj[d, x, part] + 2.0 * vel[d, x, part] for d in range(3)]
+            out = (-w[0], -(w[1] + sign * adj[3, x, part]), -w[2], -sign * adj[1, x, part])
+            for c in range(4):
+                cys[side, c, pl.ds(x, 1)] = out[c][at : at + 1]
+        return carry
+
+    lax.fori_loop(0, X, y_ends, 0, unroll=4)
 
     def energy(x, carry):
         e = None
@@ -341,16 +358,10 @@
         em[x] = jnp.where(kind[x] == 0, e, 0.0)
         return carry
 
-    lax.fori_loop(0, X, energy, 0)
-
-    def put_filt(x, v):
-        filt[x + 6] = v
-
-    def old_filt(x):
-        return filt[x + 6]
-
-    for x0, n in ((0, 6), (26, 6), (6, 10), (16, 10)):
-        yz_local(den, band, x0, n, put_filt)
+    lax.fori_loop(0, X, energy, 0, unroll=4)
+
+    for m in msg_f[2:4]:
+        m.start()
 
     lane = lanes((Y, 128))
 
@@ -387,11 +398,6 @@
         for c in range(4):
             res[c, x] = out[c]
 
-        for side, part, end, sign in ((0, plus, slice(0, 1), -0.5), (1, minus, slice(Y - 1, Y), 0.5)):
-            cys[side, 0, pl.ds(x, 1)] = -w[0][end]
-            cys[side, 1, pl.ds(x, 1)] = -part[1][end]
-            cys[side, 2, pl.ds(x, 1)] = -w[2][end]
-            cys[side, 3, pl.ds(x, 1)] = sign * lam[1][end]
         zs0 = (-w[0], -w[1], -plus[2], -0.5 * lam[2])
         zs1 = (-w[0], -w[1], -minus[2], 0.5 * lam[2])
         for c in range(4):
@@ -404,7 +410,7 @@
 
     ends = (jnp.zeros((Y, 128), f32), jnp.zeros((Y, 128), f32))
     ends = stencil(0, ends, False, True)
-    ends = lax.fori_loop(1, 12, lambda x, c: stencil(x, c, True, True), ends)
+    ends = lax.fori_loop(1, 10, lambda x, c: stencil(x, c, True, True), ends, unroll=3)
 
     for m in msg_an + msg_az:
         m.wait_recv()
@@ -442,7 +448,7 @@
                 alpha[here] = jnp.where(k == 0, 4.0 * r - 2.0, jnp.where(k == 1, 2.0, 0.0))
             return carry
 
-        lax.fori_loop(0, Y // 8, strip, 0)
+        lax.fori_loop(0, Y // 8, strip, 0, unroll=2)
 
     def smooth_x(x, n):
         def strip(q, carry):
@@ -451,7 +457,7 @@
                 grid[x + i, pl.ds(at, 8)] = f
             return carry
 
-        lax.fori_loop(0, Y // 8, strip, 0)
+        lax.fori_loop(0, Y // 8, strip, 0, unroll=2)
 
     def put_sen(x, v):
         sen[x] = v
@@ -459,10 +465,10 @@
     for x in (6, 16):
         project(x, 10)
 
-    ends = lax.fori_loop(12, X - 1, lambda x, c: stencil(x, c, True, True), ends)
+    ends = lax.fori_loop(10, X - 1, lambda x, c: stencil(x, c, True, True), ends, unroll=3)
     ends = stencil(X - 1, ends, True, False)
     czs[0], czs[1] = ends
-    for m in msg_f[2:]:
+    for m in msg_f[4:]:
         m.start()
 
     msg_c = x_messages("c", pw)
@@ -476,12 +482,14 @@
 
     for x in (6, 16):
         smooth_x(x, 10)
+    pack_z(grid, range(6, 26), zp2, True)
+    for x0 in (6, 16):
+        yz_local(grid, band, x0, 10, put_sen)
     msg_dm = face_messages("d", grid, yf2, "m")
     for m in msg_dm:
         m.start()
-    pack_z(grid, range(6, 26), zp2, True)
-    for x0 in (6, 16):
-        yz_local(grid, band, x0, 10, put_sen)
+    for m in msg_f[:2]:
+        m.start()
 
     for m in msg_f[2:]:
         m.wait_recv()
@@ -506,24 +514,23 @@
                 res[c, x] = jnp.where(k == 3, v, r)
         return carry
 
-    lax.fori_loop(1, 12, finish, 0)
+    lax.fori_loop(1, 13, finish, 0, unroll=3)
+
     for ms in msg_c:
         for m in ms:
             m.wait_recv()
     for x in (0, 26):
         smooth_x(x, 6)
 
-    msg_dn = face_messages("d", grid, yf2, "lh")
-    for m in msg_dn:
-        m.start()
     pack_z(grid, (*range(0, 6), *range(26, 32)), zp2, False)
     msg_dz = strip_messages("d", zp2, zx2)
-    for m in msg_dz:
+    msg_dn = face_messages("d", grid, yf2, "lh")
+    for m in msg_dz + msg_dn:
         m.start()
     for x0 in (0, 26):
         yz_local(grid, band, x0, 6, put_sen)
 
-    lax.fori_loop(12, X - 1, finish, 0)
+    lax.fori_loop(13, X - 1, finish, 0, unroll=3)
     for m in msg_f[:2]:
         m.wait_recv()
     for side, x in ((0, 0), (1, X - 1)):
@@ -531,9 +538,11 @@
             res[c, x] += cxr[side, c]
         finish(x, 0)
 
-    for m in msg_dn + msg_dm + msg_dz:
+    for m in msg_an + msg_am + msg_az + sum(msg_b + msg_c, []) + msg_f:
+        m.wait_send()
+    for m in msg_dm + msg_dn + msg_dz:
         m.wait_recv()
-    for m in msg_an + msg_am + msg_az + sum(msg_b + msg_c, []) + msg_f + msg_dn + msg_dm + msg_dz:
+    for m in msg_dm + msg_dn + msg_dz:
         m.wait_send()
 
 
@@ -549,9 +558,9 @@
         sen[x] = v * CUBE
 
     out_s = []
-    for g in range(2):
-        yz_halo(yf2, zy, band, g * 16, 16, old, put)
-        part = pl.ds(g * 16, 16)
+    for g in range(4):
+        yz_halo(yf2, zy, band, g * 8, 8, old, put)
+        part = pl.ds(g * 8, 8)
         out_s.append(pltpu.make_async_copy(sen.at[part], sen_o.at[part], sems.at[1 + g]))
         out_s[-1].start()
     out_r.wait()
@@ -613,7 +622,7 @@
         scratch_shapes=[
             pltpu.VMEM(strips, f32),
             pltpu.VMEM(block, f32),
-            pltpu.SemaphoreType.DMA((3,)),
+            pltpu.SemaphoreType.DMA((5,)),
         ],
         compiler_params=pltpu.CompilerParams(vmem_limit_bytes=16 * 2**20),
     )(*near)

time: 35.4 us -> 32 us (0.904)
  the two profiles are of different devices: /device:TPU:77 before, /device:TPU:97 now
where the time goes in v4:
time: 32 us; the launch traced here: 31.9 us
  Pallas kernels  31.2 us (98%)
  between operations  0.64 us (2%)
    pallas_call x1, Pallas kernels, body(): pl.pallas_call(kernel, out_shape=(pltpu.VMEM((4, *block), f32), pltpu.VME...  28.8 us
    pallas_call x1, Pallas kernels, body(): pl.pallas_call(finish_kernel, out_shape=(jax.ShapeDtypeStruct((4, *block)...  2.37 us

profile of v4, /device:TPU:97, one launch (start us, length us, event | category | flops | bytes accessed | tf_op | source)
XLA Modules:
  0.0 31.9 jit_solution(6272515329720332404)
XLA Ops:
  0.6 28.8 %shard_map.59 = (f32[4,32,32,256]{3,2,1,0:T(8,128)S(1)}, f32[32,32,256]{2,1,0:T(8,128)S(1)}, f32[2,32,8,256]{3,2,1,0:T(8,128)S(1)}, f32[2,2,48,128]{3,2,1,0:T(8,...) custom-call(f32[32,32,256]{2,1,0:T(8,128)} %den_h.1, s32[32,32,256]{2,1,0:T(8,128)} %kind_h.1, ...), custom_call_target="tpu_custom_call" | custom-call | tf_op jit(solution)/shard_map/pallas_call | solution.py:576
  29.5 2.4 %shard_map.60 = (f32[4,32,32,256]{3,2,1,0:T(8,128)}, f32[32,32,256]{2,1,0:T(8,128)}) custom-call(f32[4,32,32,256]{3,2,1,0:T(8,128)S(1)} %get-tuple-element.8.res, f32[32,32,256]{2,1,0:T(8,128)S(1)} %get-tuple-element.9.sen_in, f32[2,32,8,256]{3,2,1,0:T(8,128)S(1)} %get-tuple-element.10.yf2, f32[2,2,48,128]{3,2,1,0:T(8,128)S(1)} %get-tuple-element.11.zx2, ...), custom_call_target="tpu_custom_call" | custom-call | tf_op jit(solution)/shard_map/pallas_call | solution.py:617

commit v5 on v4

--- a/solution.py
+++ b/solution.py
@@ -485,9 +485,6 @@
     pack_z(grid, range(6, 26), zp2, True)
     for x0 in (6, 16):
         yz_local(grid, band, x0, 10, put_sen)
-    msg_dm = face_messages("d", grid, yf2, "m")
-    for m in msg_dm:
-        m.start()
     for m in msg_f[:2]:
         m.start()
 
@@ -515,6 +512,9 @@
         return carry
 
     lax.fori_loop(1, 13, finish, 0, unroll=3)
+    msg_dm = face_messages("d", grid, yf2, "m")
+    for m in msg_dm:
+        m.start()
 
     for ms in msg_c:
         for m in ms:

time: 32 us -> 32 us (level)
  no operation moved by 1% of the time
where the time goes in v5:
time: 32 us; the launch traced here: 31.9 us
  Pallas kernels  31.2 us (98%)
  between operations  0.64 us (2%)
    pallas_call x1, Pallas kernels, body(): pl.pallas_call(kernel, out_shape=(pltpu.VMEM((4, *block), f32), pltpu.VME...  28.8 us
    pallas_call x1, Pallas kernels, body(): pl.pallas_call(finish_kernel, out_shape=(jax.ShapeDtypeStruct((4, *block)...  2.37 us

profile of v5, /device:TPU:97, one launch (start us, length us, event | category | flops | bytes accessed | tf_op | source)
XLA Modules:
  0.0 31.9 jit_solution(12559028417039127510)
XLA Ops:
  0.6 28.8 %shard_map.59 = (f32[4,32,32,256]{3,2,1,0:T(8,128)S(1)}, f32[32,32,256]{2,1,0:T(8,128)S(1)}, f32[2,32,8,256]{3,2,1,0:T(8,128)S(1)}, f32[2,2,48,128]{3,2,1,0:T(8,...) custom-call(f32[32,32,256]{2,1,0:T(8,128)} %den_h.1, s32[32,32,256]{2,1,0:T(8,128)} %kind_h.1, ...), custom_call_target="tpu_custom_call" | custom-call | tf_op jit(solution)/shard_map/pallas_call | solution.py:576
  29.5 2.4 %shard_map.60 = (f32[4,32,32,256]{3,2,1,0:T(8,128)}, f32[32,32,256]{2,1,0:T(8,128)}) custom-call(f32[4,32,32,256]{3,2,1,0:T(8,128)S(1)} %get-tuple-element.8.res, f32[32,32,256]{2,1,0:T(8,128)S(1)} %get-tuple-element.9.sen_in, f32[2,32,8,256]{3,2,1,0:T(8,128)S(1)} %get-tuple-element.10.yf2, f32[2,2,48,128]{3,2,1,0:T(8,128)S(1)} %get-tuple-element.11.zx2, ...), custom_call_target="tpu_custom_call" | custom-call | tf_op jit(solution)/shard_map/pallas_call | solution.py:617
